TPU v7x, 32 devices: a whole 2x2x4 slice. The times are simulated.
32 devices in a mesh: tensor: 2 (over x), wide: 16 (over z, y, core).
Axes of the slice: x: 2, y: 2, z: 4, core: 2. Of those that a mesh axis runs over, the one named last changes fastest.
Arguments:
- tokens: bfloat16 [128, 3072], P('wide', 'tensor'), may hold values from -6 to 6
- cotangent: bfloat16 [128, 3072], P('wide', 'tensor'), may hold values from -1.5 to 1.5
- gates: bfloat16 [128, 2], P('wide'), may hold values from 0.19921875 to 1
- experts: int32 [128, 2], P('wide'), may hold values from 0 to 7, all different within a row; in each aligned block of 8 rows (0 to 7, 8 to 15, ...) at most 4 rows name the same one
- w_gate: bfloat16 [16, 3072, 4096], P('wide', None, 'tensor'), may hold values from -0.109375 to 0.109375
- w_up: bfloat16 [16, 3072, 4096], P('wide', None, 'tensor'), may hold values from -0.109375 to 0.109375
- w_down: bfloat16 [16, 4096, 3072], P('wide', 'tensor'), may hold values from -0.0625 to 0.0625
Outputs:
- input_grad: bfloat16 [128, 3072], P('wide', 'tensor')
- routing_grad: float32 [128, 2], P('wide')
- gate_proj_grad: bfloat16 [16, 3072, 4096], P('wide', None, 'tensor')
- up_proj_grad: bfloat16 [16, 3072, 4096], P('wide', None, 'tensor')
- down_proj_grad: bfloat16 [16, 4096, 3072], P('wide', 'tensor')
Inputs may be any that keep to these rules, and one draw needn't show every extreme that they name: Each token names 2 different experts. Among the 8 tokens of one index of wide (aligned blocks of rows) no expert is named more than 4 times, and in every draw some expert is named exactly 4 times by some block.
All inputs are finite; a program needn't handle non-finite values.
Results may differ from a plain program's by a relative error of at most 0.02.
Values may be sent and summed in bfloat16 or wider, within the bound.
No kernel may reach another device: no remote copies, remote signals or barrier semaphores. Data moves between devices by JAX's collectives and lax.ppermute only.
A program may use at most 128 MiB of HBM per device.

v0:
```python
import jax
import jax.numpy as jnp
from jax import lax
from jax.sharding import PartitionSpec as P

E = 8
CAP = 4


def contract_rows(left_side, right_side):
    return lax.dot_general(
        left_side, right_side, (((0,), (0,)), ((), ())), preferred_element_type=jnp.float32
    )


def contract_cols(left_side, right_side):
    return lax.dot_general(
        left_side, right_side, (((1,), (1,)), ((), ())), preferred_element_type=jnp.float32
    )


def shards(tokens, cotangent, gates, experts, w_gate, w_up, w_down):
    n_wide = lax.axis_size("wide")
    replicas = n_wide // E
    tok_count = tokens.shape[0]
    feature_width = w_gate.shape[1]
    slot_rows = n_wide * CAP
    chosen = experts[:, :, None] == jnp.arange(E, dtype=jnp.int32)[None, None, :]
    picked = jnp.sum(chosen.astype(jnp.int32), axis=1)
    before = jnp.cumsum(picked, axis=0) - picked
    slot_table = (picked[:, :, None] == 1) & (
        before[:, :, None] == jnp.arange(CAP, dtype=jnp.int32)[None, None, :]
    )
    route_matrix = slot_table.reshape(tok_count, E * CAP).astype(jnp.bfloat16)
    gate_each = jnp.sum(jnp.where(chosen, gates[:, :, None].astype(jnp.float32), 0.0), axis=1)
    slot_gate = jnp.sum(jnp.where(slot_table, gate_each[:, :, None], 0.0), axis=0).astype(
        jnp.bfloat16
    )
    gate_sent = jnp.broadcast_to(slot_gate.reshape(E, 1, CAP), (E, replicas, CAP)).reshape(
        n_wide, CAP
    )

    def spread(slot_block):
        columns = slot_block.shape[-1]
        widened = jnp.broadcast_to(
            slot_block.reshape(E, 1, CAP, columns), (E, replicas, CAP, columns)
        )
        return widened.reshape(n_wide, CAP, columns)

    def select(source):
        return contract_rows(route_matrix, source).astype(jnp.bfloat16)

    full_in, full_up = (
        lax.all_gather(tokens, "tensor", axis=1, tiled=True),
        lax.all_gather(cotangent, "tensor", axis=1, tiled=True),
    )
    got_in, got_up, got_gate = (
        lax.all_to_all(spread(select(full_in)), "wide", split_axis=0, concat_axis=0, tiled=True),
        lax.all_to_all(spread(select(full_up)), "wide", split_axis=0, concat_axis=0, tiled=True),
        lax.all_to_all(gate_sent, "wide", split_axis=0, concat_axis=0, tiled=True),
    )
    inputs = got_in.reshape(slot_rows, feature_width)
    upstream = got_up.reshape(slot_rows, feature_width)
    slot_scale = got_gate.reshape(slot_rows).astype(jnp.float32)
    w_first = w_gate[0]
    w_second = w_up[0]
    w_out = w_down[0]
    pre_gate = jnp.dot(inputs, w_first, preferred_element_type=jnp.float32)
    pre_up = jnp.dot(inputs, w_second, preferred_element_type=jnp.float32)
    sigmoid_gate = jax.nn.sigmoid(pre_gate)
    active = pre_gate * sigmoid_gate
    hidden = active * pre_up
    weighted = (slot_scale[:, None] * hidden).astype(jnp.bfloat16)
    through = contract_cols(upstream, w_out)
    gate_terms = lax.psum(jnp.sum(through * hidden, axis=1), "tensor")
    hidden_grad = slot_scale[:, None] * through
    grad_pre_gate = (
        hidden_grad * pre_up * sigmoid_gate * (1.0 + pre_gate * (1.0 - sigmoid_gate))
    ).astype(jnp.bfloat16)
    grad_pre_up = (hidden_grad * active).astype(jnp.bfloat16)
    gate_proj_grad = contract_rows(inputs, grad_pre_gate).astype(jnp.bfloat16)[None]
    up_proj_grad = contract_rows(inputs, grad_pre_up).astype(jnp.bfloat16)[None]
    down_proj_grad = contract_rows(weighted, upstream).astype(jnp.bfloat16)[None]
    returned = contract_cols(grad_pre_gate, w_first) + contract_cols(grad_pre_up, w_second)
    back_rows, back_gate = (
        lax.all_to_all(
            returned.reshape(n_wide, CAP, feature_width).astype(jnp.bfloat16),
            "wide",
            split_axis=0,
            concat_axis=0,
            tiled=True,
        ).astype(jnp.float32),
        lax.all_to_all(
            gate_terms.reshape(n_wide, CAP).astype(jnp.bfloat16),
            "wide",
            split_axis=0,
            concat_axis=0,
            tiled=True,
        ).astype(jnp.float32),
    )
    summed_rows = jnp.sum(back_rows.reshape(E, replicas, CAP, feature_width), axis=1).reshape(
        E * CAP, feature_width
    )
    summed_gate = jnp.sum(back_gate.reshape(E, replicas, CAP), axis=1)
    full_grad = jnp.dot(
        route_matrix.astype(jnp.float32), summed_rows, precision=lax.Precision.HIGHEST
    )
    input_grad = lax.psum_scatter(
        full_grad.astype(jnp.bfloat16), "tensor", scatter_dimension=1, tiled=True
    )
    per_expert = jnp.sum(jnp.where(slot_table, summed_gate[None, :, :], 0.0), axis=2)
    routing_grad = jnp.sum(jnp.where(chosen, per_expert[:, None, :], 0.0), axis=2)
    return (input_grad, routing_grad, gate_proj_grad, up_proj_grad, down_proj_grad)


def solution(mesh):
    return jax.shard_map(
        shards,
        mesh=mesh,
        in_specs=(
            P("wide", "tensor"),
            P("wide", "tensor"),
            P("wide", None),
            P("wide", None),
            P("wide", None, "tensor"),
            P("wide", None, "tensor"),
            P("wide", "tensor", None),
        ),
        out_specs=(
            P("wide", "tensor"),
            P("wide", None),
            P("wide", None, "tensor"),
            P("wide", None, "tensor"),
            P("wide", "tensor", None),
        ),
        check_vma=False,
    )
```

profile of v0, /device:TPU:0, one launch (start us, length us, event | category | flops | bytes accessed | tf_op | source)
XLA Modules:
  0.0 140.6 jit_solution(4430772225419627302)
XLA Ops:
  7.2 0.8 convert_reduce_fusion.2
  8.2 5.7 %all_gather.7 = bf16[8,3072]{1,0:T(8,128)(2,1)S(1)} all-gather(bf16[8,1536]{1,0:T(8,128)(2,1)} %param.7), channel_id=1, replica_groups=mesh['tensor'=2,'wide'=16] {'tensor'}, dimensions={1}, use_global_device_ids=true | all-gather | bytes 73728 | tf_op jit(solution)/shard_map/all_gather | solution.py:54
  14.2 0.9 broadcast_in_dim.91
  15.1 6.4 %all-to-all-start.2 = ((bf16[16,4,3072]{2,1,0:T(4,128)(2,1)}), bf16[16,4,3072]{2,1,0:T(4,128)(2,1)S(1)}, u32[]{:S(2)}, u32[]{:S(2)}) async-start(bf16[16,4,3072]{2,1,0:T(4,128)(2,1)} %bitcast.5), calls=%async_computation.2 | async-start | bytes 786432 | tf_op jit(solution)/shard_map/all_to_all | solution.py:58
  21.5 0.7 convert_element_type.85
  22.2 4.7 %all_gather.6 = bf16[8,3072]{1,0:T(8,128)(2,1)S(1)} all-gather(bf16[8,1536]{1,0:T(8,128)(2,1)} %param.8), channel_id=1, replica_groups=mesh['tensor'=2,'wide'=16] {'tensor'}, dimensions={1}, use_global_device_ids=true | all-gather | bytes 73728 | tf_op jit(solution)/shard_map/all_gather | solution.py:55
  27.2 6.6 %all-to-all-done.2 = bf16[16,4,3072]{2,1,0:T(4,128)(2,1)S(1)} async-done(((bf16[16,4,3072]{2,1,0:T(4,128)(2,1)}), bf16[16,4,3072]{2,1,0:T(4,128)(2,1)S(1)}, u32[]{:S(2)}, u32[]{:S(2)}) %all-to-all-start.2) | async-done | bytes 393248 | tf_op jit(solution)/shard_map/all_to_all | solution.py:58
  33.7 0.9 broadcast_in_dim.89
  34.6 3.6 %all-to-all-start.1 = ((bf16[16,4,3072]{2,1,0:T(4,128)(2,1)}), bf16[16,4,3072]{2,1,0:T(4,128)(2,1)S(1)}, u32[]{:S(2)}, u32[]{:S(2)}) async-start(bf16[16,4,3072]{2,1,0:T(4,128)(2,1)} %bitcast.3), calls=%async_computation.1 | async-start | bytes 786432 | tf_op jit(solution)/shard_map/all_to_all | solution.py:59
  38.3 7.0 %fusion.2 = f32[64,2048]{1,0:T(8,128)S(1)} fusion(bf16[64,3072]{1,0:T(8,128)(2,1)S(1)} %reshape.96, bf16[1,3072,2048]{2,1,0:T(8,128)(2,1)} %param.11), kind=kOutput, calls=%fused_computation.2 | convolution fusion | flops 805306368 | bytes 13500416 | tf_op jit(solution)/shard_map/dot_general | solution.py:68
  45.3 1.1 copy-done
  46.4 2.3 %fusion.6 = f32[64,2048]{1,0:T(8,128)S(1)} fusion(bf16[64,3072]{1,0:T(8,128)(2,1)S(1)} %reshape.96, bf16[1,3072,2048]{2,1,0:T(8,128)(2,1)S(1)} %copy-done), kind=kOutput, calls=%fused_computation.6 | convolution fusion | flops 805306368 | bytes 13500416 | tf_op jit(solution)/shard_map/dot_general | solution.py:69
  48.7 1.6 %all-to-all-done.1 = bf16[16,4,3072]{2,1,0:T(4,128)(2,1)S(1)} async-done(((bf16[16,4,3072]{2,1,0:T(4,128)(2,1)}), bf16[16,4,3072]{2,1,0:T(4,128)(2,1)S(1)}, u32[]{:S(2)}, u32[]{:S(2)}) %all-to-all-start.1) | async-done | bytes 393248 | tf_op jit(solution)/shard_map/all_to_all | solution.py:59
  50.4 8.6 %multiply_reduce_fusion = (f32[64]{0:T(128)S(1)}, f32[64,2048]{1,0:T(8,128)S(1)}) fusion(f32[64,2048]{1,0:T(8,128)S(1)} %fusion.6, f32[64,2048]{1,0:T(8,128)S(1)} %fusion.2, bf16[64,3072]{1,0:T(8,128)(2,1)S(1)} %reshape.94, bf16[1,2048,3072]{2,1,0:T(8,128)(2,1)} %param.13), kind=kOutput, calls=%fused_computation.21 | convolution fusion | flops 806223808 | bytes 14549248 | tf_op jit(solution)/shard_map/dot_general | solution.py:17
  59.0 4.9 %psum.7 = bf16[64]{0:T(256)(128)(2,1)S(1)} all-reduce(f32[64]{0:T(128)S(1)} %get-tuple-element.9), channel_id=1, replica_groups=mesh['tensor'=2,'wide'=16] {'tensor'}, use_global_device_ids=true, to_apply=%region_7.8 | all-reduce | flops 64 | bytes 384 | tf_op jit(solution)/shard_map/psum | solution.py:75
  64.0 0.7 convert_element_type.106
  64.7 4.4 %all-to-all-start.4 = ((bf16[16,1,4]{2,1,0:T(2,128)(2,1)}), bf16[16,1,4]{2,1,0:T(2,128)(2,1)S(1)}, u32[]{:S(2)}, u32[]{:S(2)}) async-start(bf16[16,1,4]{2,1,0:T(2,128)(2,1)} %convert_element_type.106), calls=%async_computation.5 | async-start | bytes 16384 | tf_op jit(solution)/shard_map/all_to_all | solution.py:93
  69.2 6.2 %all-to-all-done.4 = bf16[16,1,4]{2,1,0:T(2,128)(2,1)S(1)} async-done(((bf16[16,1,4]{2,1,0:T(2,128)(2,1)}), bf16[16,1,4]{2,1,0:T(2,128)(2,1)S(1)}, u32[]{:S(2)}, u32[]{:S(2)}) %all-to-all-start.4) | async-done | bytes 160 | tf_op jit(solution)/shard_map/all_to_all | solution.py:93
  75.6 0.6 copy.25
  76.3 3.7 %all-to-all-start = ((bf16[16,1,4]{2,1,0:T(2,128)(2,1)}), bf16[16,1,4]{2,1,0:T(2,128)(2,1)S(1)}, u32[]{:S(2)}, u32[]{:S(2)}) async-start(bf16[16,1,4]{2,1,0:T(2,128)(2,1)} %copy.25), calls=%async_computation | async-start | bytes 16384 | tf_op jit(solution)/shard_map/all_to_all | solution.py:60
  79.9 0.7 select_reduce_fusion.2
  80.6 5.4 %all-to-all-done = bf16[16,1,4]{2,1,0:T(2,128)(2,1)S(1)} async-done(((bf16[16,1,4]{2,1,0:T(2,128)(2,1)}), bf16[16,1,4]{2,1,0:T(2,128)(2,1)S(1)}, u32[]{:S(2)}, u32[]{:S(2)}) %all-to-all-start) | async-done | bytes 160 | tf_op jit(solution)/shard_map/all_to_all | solution.py:60
  86.1 0.3 multiply_convert_fusion.1
  86.4 8.5 %fusion = f32[64,3072]{1,0:T(8,128)S(1)} fusion(bf16[64,2048]{1,0:T(8,128)(2,1)S(1)} %get-tuple-element.8, bf16[1,3072,2048]{2,1,0:T(8,128)(2,1)} %param.11), kind=kOutput, calls=%fused_computation | convolution fusion | flops 805306368 | bytes 13631488 | tf_op jit(solution)/shard_map/dot_general | solution.py:17
  94.9 8.5 %fusion.13 = bf16[64,3072]{1,0:T(8,128)(2,1)S(1)} fusion(f32[64,3072]{1,0:T(8,128)S(1)} %fusion, bf16[64,2048]{1,0:T(8,128)(2,1)S(1)} %get-tuple-element.7, bf16[1,3072,2048]{2,1,0:T(8,128)(2,1)} %param.12), kind=kOutput, calls=%fused_computation.14 | convolution fusion | flops 805699584 | bytes 14024704 | tf_op jit(solution)/shard_map/dot_general | solution.py:17
  103.4 0.9 convert_element_type.94
  104.3 3.6 %all-to-all-start.3 = ((bf16[16,4,3072]{2,1,0:T(4,128)(2,1)}), bf16[16,4,3072]{2,1,0:T(4,128)(2,1)S(1)}, u32[]{:S(2)}, u32[]{:S(2)}) async-start(bf16[16,4,3072]{2,1,0:T(4,128)(2,1)} %convert_element_type.94), calls=%async_computation.3 | async-start | bytes 786432 | tf_op jit(solution)/shard_map/all_to_all | solution.py:86
  107.9 6.6 %convert_bitcast_fusion.1 = bf16[1,3072,2048]{2,1,0:T(8,128)(2,1)} fusion(bf16[64,3072]{1,0:T(8,128)(2,1)S(1)} %reshape.96, bf16[64,2048]{1,0:T(8,128)(2,1)S(1)} %get-tuple-element.7), kind=kOutput, calls=%fused_computation.11 | convolution fusion | flops 811597824 | bytes 13238272 | tf_op jit(solution)/shard_map/dot_general | solution.py:11
  114.6 6.7 %convert_bitcast_fusion = bf16[1,2048,3072]{2,1,0:T(8,128)(2,1)} fusion(bf16[64,3072]{1,0:T(8,128)(2,1)S(1)} %reshape.94, f32[64]{0:T(128)S(1)} %reshape.99, f32[64,2048]{1,0:T(8,128)S(1)} %fusion.6, f32[64,2048]{1,0:T(8,128)S(1)} %fusion.2), kind=kOutput, calls=%fused_computation.10 | convolution fusion | flops 812515328 | bytes 14024960 | tf_op jit(solution)/shard_map/dot_general | solution.py:11
  121.5 1.0 fusion.16
  122.5 6.6 %convert_bitcast_fusion.2 = bf16[1,3072,2048]{2,1,0:T(8,128)(2,1)} fusion(bf16[64,3072]{1,0:T(8,128)(2,1)S(1)} %reshape.96, bf16[64,2048]{1,0:T(8,128)(2,1)S(1)} %get-tuple-element.8), kind=kOutput, calls=%fused_computation.12 | convolution fusion | flops 811597824 | bytes 13238272 | tf_op jit(solution)/shard_map/dot_general | solution.py:11
  129.1 4.7 %reduce-scatter.2.cloned.1.call-done = bf16[8,1536]{1,0:T(8,128)(2,1)} async-done(((bf16[8,3072]{1,0:T(8,128)(2,1)}), bf16[8,1536]{1,0:T(8,128)(2,1)}) %reduce-scatter.2.cloned.1.call-update) | async-done | bytes 24592 | tf_op jit(solution)/shard_map/reduce_scatter | solution.py:108
  (32 shorter events, 1.8 us)
Async XLA Ops:
  15.1 18.6 %all-to-all-start.2 = ((bf16[16,4,3072]{2,1,0:T(4,128)(2,1)}), bf16[16,4,3072]{2,1,0:T(4,128)(2,1)S(1)}, u32[]{:S(2)}, u32[]{:S(2)}) async-start(bf16[16,4,3072]{2,1,0:T(4,128)(2,1)} %bitcast.5), calls=%async_computation.2 | async-start | bytes 786432 | tf_op jit(solution)/shard_map/all_to_all | solution.py:58
  34.6 15.7 %all-to-all-start.1 = ((bf16[16,4,3072]{2,1,0:T(4,128)(2,1)}), bf16[16,4,3072]{2,1,0:T(4,128)(2,1)S(1)}, u32[]{:S(2)}, u32[]{:S(2)}) async-start(bf16[16,4,3072]{2,1,0:T(4,128)(2,1)} %bitcast.3), calls=%async_computation.1 | async-start | bytes 786432 | tf_op jit(solution)/shard_map/all_to_all | solution.py:59
  38.3 8.2 %copy-start = (bf16[1,3072,2048]{2,1,0:T(8,128)(2,1)S(1)}, bf16[1,3072,2048]{2,1,0:T(8,128)(2,1)}, u32[]{:S(2)}) copy-start(bf16[1,3072,2048]{2,1,0:T(8,128)(2,1)} %param.12) | copy-start | bytes 37748740
  48.7 20.4 %copy-start.1 = (s32[8,2]{0,1:T(2,128)S(1)}, s32[8,2]{0,1:T(2,128)}, u32[]{:S(2)}) copy-start(s32[8,2]{0,1:T(2,128)} %param.10) | copy-start | bytes 196
  64.7 10.7 %all-to-all-start.4 = ((bf16[16,1,4]{2,1,0:T(2,128)(2,1)}), bf16[16,1,4]{2,1,0:T(2,128)(2,1)S(1)}, u32[]{:S(2)}, u32[]{:S(2)}) async-start(bf16[16,1,4]{2,1,0:T(2,128)(2,1)} %convert_element_type.106), calls=%async_computation.5 | async-start | bytes 16384 | tf_op jit(solution)/shard_map/all_to_all | solution.py:93
  76.3 9.8 %all-to-all-start = ((bf16[16,1,4]{2,1,0:T(2,128)(2,1)}), bf16[16,1,4]{2,1,0:T(2,128)(2,1)S(1)}, u32[]{:S(2)}, u32[]{:S(2)}) async-start(bf16[16,1,4]{2,1,0:T(2,128)(2,1)} %copy.25), calls=%async_computation | async-start | bytes 16384 | tf_op jit(solution)/shard_map/all_to_all | solution.py:60
  104.3 16.9 %all-to-all-start.3 = ((bf16[16,4,3072]{2,1,0:T(4,128)(2,1)}), bf16[16,4,3072]{2,1,0:T(4,128)(2,1)S(1)}, u32[]{:S(2)}, u32[]{:S(2)}) async-start(bf16[16,4,3072]{2,1,0:T(4,128)(2,1)} %convert_element_type.94), calls=%async_computation.3 | async-start | bytes 786432 | tf_op jit(solution)/shard_map/all_to_all | solution.py:86
  107.9 25.9 %reduce-scatter.2.cloned.1.call-start = ((), (), s32[]{:S(2)}) async-start(), calls=%async_computation.6 | async-start | bytes 73728 | tf_op jit(solution)/shard_map/reduce_scatter | solution.py:108
Sparse Core Ops, SparseCore 0:
  122.6 11.1 reduce-scatter.1
where the time goes:
time: 141 us
  matrix products  56.2 us (40%)
  waiting for transfers between devices  24.4 us (17%)
  starting transfers between devices  21.6 us (15%)
  blocking collectives  15.3 us (11%)
  between operations  14.2 us (10%)
  local copies, waits for them, and re-layouts  5.91 us (4%)
  other arithmetic  2.99 us (2%)
    dot_general x3, matrix products, contract_cols(): lax.dot_general(left_side, right_side, (((1,), (1,)), ((), ())), preferre...  25.6 us
    dot_general x5, matrix products, contract_rows(): lax.dot_general(left_side, right_side, (((0,), (0,)), ((), ())), preferre...  20.3 us
    dot_general x1, matrix products, shards(): pre_gate = jnp.dot(inputs, w_first, preferred_element_type=jnp.float32)  7.02 us
    all_to_all x1, waiting for transfers between devices, shards(): lax.all_to_all(spread(select(full_in)), 'wide', split_axis=0, concat_axis...  6.56 us
    all_to_all x1, starting transfers between devices, shards(): lax.all_to_all(spread(select(full_in)), 'wide', split_axis=0, concat_axis...  6.43 us
    all_to_all x1, waiting for transfers between devices, shards(): lax.all_to_all(gate_terms.reshape(n_wide, CAP).astype(jnp.bfloat16), 'wid...  6.17 us
    all_gather x1, blocking collectives, shards(): lax.all_gather(tokens, 'tensor', axis=1, tiled=True)  5.66 us
    all_to_all x1, waiting for transfers between devices, shards(): lax.all_to_all(gate_sent, 'wide', split_axis=0, concat_axis=0, tiled=True)  5.4 us
  transfers between devices with their start and end apart: 6, of which 5 were waited for; matrix products, arithmetic and copies ran while one was open for 22% of the time, Pallas kernels for 0%

commit v1 on v0

v1 whole, which is shorter than its diff:
```python
import functools

import jax
import jax.numpy as jnp
from jax import lax
from jax.experimental import pallas as pl
from jax.experimental.pallas import tpu as pltpu
from jax.sharding import PartitionSpec as P

E = 8
CAP = 4
LANES = 128
BF = jnp.bfloat16
F32 = jnp.float32
VMEM = pl.BlockSpec(memory_space=pltpu.VMEM)
SMEM = pl.BlockSpec(memory_space=pltpu.SMEM)
ANY = pl.BlockSpec(memory_space=pl.ANY)


def dot(left, right, left_dim, right_dim):
    return lax.dot_general(
        left, right, (((left_dim,), (right_dim,)), ((), ())), preferred_element_type=F32
    )


def params(mib):
    return pltpu.CompilerParams(vmem_limit_bytes=mib << 20)


def cost(flops, moved):
    return pl.CostEstimate(flops=flops, bytes_accessed=moved, transcendentals=0)


def column(row):
    n = row.shape[1]
    sub = lax.broadcasted_iota(jnp.int32, (n, n), 0)
    lane = lax.broadcasted_iota(jnp.int32, (n, n), 1)
    return jnp.sum(jnp.where(sub == lane, jnp.broadcast_to(row, (n, n)), 0.0), axis=1, keepdims=True)


def routing(experts_ref, lane_expert):
    ids = experts_ref[...].astype(F32)
    first, second = column(ids[0:1, :]), column(ids[1:2, :])
    hit_first = lane_expert == first
    hit_second = lane_expert == second
    picked = jnp.where(hit_first | hit_second, 1.0, 0.0)
    sub = lax.broadcasted_iota(jnp.int32, picked.shape, 0)
    before = jnp.zeros_like(picked)
    for row in range(picked.shape[0] - 1):
        before = before + jnp.where(sub > row, picked[row : row + 1, :], 0.0)
    return hit_first, hit_second, picked, before


def pack_kernel(tokens_ref, cotangent_ref, gates_ref, experts_ref, out_ref):
    width = tokens_ref.shape[1]
    rows = tokens_ref.shape[0]
    lane = lax.broadcasted_iota(jnp.int32, (rows, LANES), 1)
    lane_expert = (lane % E).astype(F32)
    hit_first, hit_second, picked, before = routing(experts_ref, lane_expert)
    gates = gates_ref[...].astype(F32)
    gate = jnp.where(hit_first, column(gates[0:1, :]), 0.0) + jnp.where(
        hit_second, column(gates[1:2, :]), 0.0
    )
    place = jnp.where(picked > 0.5, before, -1.0)
    info = jnp.where(lane < E, place, jnp.where(lane < 2 * E, gate, 0.0))
    out_ref[:, :width] = tokens_ref[...]
    out_ref[:, width : 2 * width] = cotangent_ref[...]
    out_ref[:, 2 * width :] = info.astype(BF)


def stage_kernel(parts, position_ref, after_ref, source_ref, out_ref, token_ref, sems):
    width = out_ref.shape[0] // len(parts)
    copies = []
    for i, mask in enumerate(parts):
        start = pl.multiple_of((position_ref[0] ^ mask) * width, width)
        copies.append(
            pltpu.make_async_copy(
                source_ref.at[pl.ds(start, width)], out_ref.at[pl.ds(i * width, width)], sems.at[i]
            )
        )
    for copy in copies:
        copy.start()
    token_ref[...] = jnp.zeros_like(token_ref)
    for copy in copies:
        copy.wait()


def stage(position, weight, parts, width, after):
    rows, columns = width * len(parts), weight.shape[1]
    return pl.pallas_call(
        functools.partial(stage_kernel, parts),
        out_shape=[pltpu.VMEM((rows, columns), BF), pltpu.VMEM((8, LANES), F32)],
        in_specs=[SMEM, ANY, ANY],
        out_specs=[ANY, VMEM],
        scratch_shapes=[pltpu.SemaphoreType.DMA((len(parts),))],
        compiler_params=params(4),
        cost_estimate=cost(0, 4 * rows * columns),
        name="stage",
    )(position, after, pltpu.with_memory_space_constraint(weight, pltpu.HBM))


def join_kernel(own_ref, got_ref, *refs):
    out_ref = refs[-1]
    rows = own_ref.shape[0]
    out_ref[:rows, :] = own_ref[...]
    out_ref[rows:, :] = got_ref[...]


def select_kernel(expert_ref, own_ref, got_ref, *refs):
    out_ref = refs[-1]
    expert = expert_ref[0]
    tok_rows, full = own_ref.shape
    slots = out_ref.shape[0]
    blocks = slots // CAP // 2
    per_block = tok_rows // blocks
    total = jnp.zeros((slots, full), F32)
    for side, ref in enumerate((own_ref, got_ref)):
        info = ref[:, full - LANES :].astype(F32)
        lane = lax.broadcasted_iota(jnp.int32, info.shape, 1)
        place = jnp.sum(jnp.where(lane == expert, info, 0.0), axis=1, keepdims=True)
        row = lax.broadcasted_iota(jnp.int32, (tok_rows, slots), 0)
        col = lax.broadcasted_iota(jnp.int32, (tok_rows, slots), 1)
        take = (row // per_block + side * blocks == col // CAP) & (place == (col % CAP).astype(F32))
        total = total + dot(jnp.where(take, 1.0, 0.0).astype(BF), ref[...], 0, 0)
    out_ref[...] = total.astype(BF)


def stacked(refs, start, size):
    return jnp.concatenate([ref[:, start : start + size] for ref in refs], axis=0)


def down_copies(tiles, tile, places, w_down, buffer, sems):
    return [
        [
            pltpu.make_async_copy(
                w_down.at[pl.ds(i * tile, tile), place], buffer.at[m, pl.ds(i * tile, tile)], sems.at[m, i]
            )
            for m, place in enumerate(places)
        ]
        for i in range(tiles)
    ]


def first_kernel(replicas, position_ref, *refs):
    parts = refs[:replicas]
    w_gate, w_up, w_down, gate_out, up_out, through_out, buffer, sems = refs[replicas:]
    width = (parts[0].shape[1] - LANES) // 2
    here = pl.ds(pl.multiple_of(position_ref[0] * width, width), width)
    hidden = w_gate.shape[1]
    tiles = sems.shape[1]
    tile = hidden // tiles
    copies = down_copies(tiles, tile, [here], w_down, buffer, sems)
    for row in copies:
        row[0].start()
    inputs = stacked(parts, 0, width)
    upstream = stacked(parts, width, width)
    for i in range(tiles):
        units = slice(i * tile, (i + 1) * tile)
        gate_out[:, units] = dot(inputs, w_gate[:, units], 1, 0)
        up_out[:, units] = dot(inputs, w_up[:, units], 1, 0)
        copies[i][0].wait()
        through_out[:, units] = dot(upstream, buffer[0, units, :], 1, 1)


def second_kernel(replicas, others, position_ref, *refs):
    own = refs[:replicas]
    parts = [refs[replicas * (m + 1) : replicas * (m + 2)] for m in range(others)]
    rest = refs[replicas * (others + 1) :]
    w_gate, w_up, w_down, gate_in, up_in, through_in = rest[:6]
    weighted_ref, grad_gate_ref, grad_up_ref, inputs_ref, upstream_ref, routing_ref = rest[6:12]
    buffer, sems = rest[12:]
    full = own[0].shape[1]
    width = (full - LANES) // 2
    position, expert = position_ref[0], position_ref[1]
    places = [pl.ds(pl.multiple_of((position ^ m) * width, width), width) for m in range(others + 1)]
    hidden = w_gate.shape[1]
    tiles = sems.shape[1]
    tile = hidden // tiles
    copies = down_copies(tiles, tile, places[1:], w_down, buffer, sems)
    for row in copies:
        for copy in row:
            copy.start()
    info = stacked(own, full - LANES, LANES).astype(F32)
    lane = lax.broadcasted_iota(jnp.int32, info.shape, 1)
    scale = jnp.sum(jnp.where(lane == expert + E, info, 0.0), axis=1, keepdims=True)
    for m, blocks in enumerate([own] + parts):
        inputs_ref[:, places[m]] = stacked(blocks, 0, width)
        upstream_ref[:, places[m]] = stacked(blocks, width, width)
    x = jnp.concatenate([stacked(part, 0, width) for part in parts], axis=1)
    score = jnp.zeros_like(routing_ref)
    for i in range(tiles):
        units = slice(i * tile, (i + 1) * tile)
        pre_gate = gate_in[:, units] + dot(x, w_gate[:, units], 1, 0)
        pre_up = up_in[:, units] + dot(x, w_up[:, units], 1, 0)
        through = through_in[:, units]
        for m in range(others):
            copies[i][m].wait()
            through = through + dot(stacked(parts[m], width, width), buffer[m, units, :], 1, 1)
        sig = jax.nn.sigmoid(pre_gate)
        act = pre_gate * sig
        product = act * pre_up
        weighted_ref[:, units] = (scale * product).astype(BF)
        score = score + jnp.sum(through * product, axis=1, keepdims=True)
        scaled = scale * through
        grad_gate_ref[:, units] = (scaled * pre_up * sig * (1.0 + pre_gate * (1.0 - sig))).astype(BF)
        grad_up_ref[:, units] = (scaled * act).astype(BF)
    routing_ref[...] = score


def halves(value, shape):
    high = value.astype(BF).astype(F32)
    lane = lax.broadcasted_iota(jnp.int32, shape, 1)
    return jnp.where(lane == 0, high, jnp.where(lane == 1, value - high, 0.0)).astype(BF)


def joined(lanes):
    lane = lax.broadcasted_iota(jnp.int32, lanes.shape, 1)
    return jnp.sum(jnp.where(lane < 2, lanes.astype(F32), 0.0), axis=1, keepdims=True)


def back_kernel(grad_gate, grad_up, w_gate, w_up, routing_ref, out_ref):
    width = w_gate.shape[0]
    part = dot(w_gate[...], grad_gate[...], 1, 1) + dot(w_up[...], grad_up[...], 1, 1)
    out_ref[:, :width] = part.astype(out_ref.dtype).T
    if out_ref.shape[1] > width:
        out_ref[:, width:] = halves(routing_ref[...], (out_ref.shape[0], LANES))


def back_other_kernel(others, *refs):
    grad_gate, grad_up, w_gate, w_up, routing_ref = refs[:5]
    outs = refs[5:]
    width = w_gate.shape[0] // others
    for m, out_ref in enumerate(outs):
        rows = pl.ds(m * width, width)
        back_kernel(grad_gate, grad_up, w_gate.at[rows], w_up.at[rows], routing_ref, out_ref)


def merge_kernel(replicas, offsets, position_ref, own_ref, routing_ref, *refs):
    parts, out_ref = refs[:-1], refs[-1]
    slots, width = own_ref.shape
    half = out_ref.shape[1]
    total = own_ref[...]
    score = routing_ref[...]
    for part in parts:
        total = total + part[:, :width].astype(F32)
        score = score + joined(part[:, width:])
    rows = jnp.concatenate(
        [total.astype(BF), halves(score, (slots, 2 * half - width))], axis=1
    )
    place = position_ref[2]
    out_row = lax.broadcasted_iota(jnp.int32, (2 * slots, slots), 0)
    slot = lax.broadcasted_iota(jnp.int32, (2 * slots, slots), 1)
    blocks = len(offsets)
    origin = jnp.zeros_like(slot)
    for r in range(replicas):
        for j, offset in enumerate(offsets):
            origin = jnp.where(slot // CAP == r * blocks + j, offset ^ r, origin)
    origin = origin ^ place
    lands = (out_row // (2 * CAP) == origin) & (out_row % CAP == slot % CAP)
    low = lands & (out_row % (2 * CAP) < CAP)
    high = lands & (out_row % (2 * CAP) >= CAP)
    out = dot(jnp.where(low, 1.0, 0.0).astype(BF), rows[:, :half], 1, 0)
    out = out + dot(jnp.where(high, 1.0, 0.0).astype(BF), rows[:, half:], 1, 0)
    out_ref[...] = out.astype(BF)


def finish_kernel(replicas, back_ref, experts_ref, grad_ref, routing_ref):
    rows, half = back_ref.shape
    tok, width = grad_ref.shape
    lane = lax.broadcasted_iota(jnp.int32, (tok, rows), 1)
    lane_expert = ((lane // (2 * CAP)) // replicas).astype(F32)
    hit_first, hit_second, _, before = routing(experts_ref, lane_expert)
    here = before == (lane % CAP).astype(F32)
    low = lane % (2 * CAP) < CAP
    any_hit = (hit_first | hit_second) & here

    def gather(mask, part):
        return dot(jnp.where(mask, 1.0, 0.0).astype(BF), part, 1, 0)

    grad_ref[:, :half] = gather(any_hit & low, back_ref[...]).astype(BF)
    tail = back_ref[:, : width - half]
    grad_ref[:, half:] = gather(any_hit & ~low, tail).astype(BF)
    score = back_ref[:, width - half : width - half + LANES]
    outs = [joined32(gather(hit & here & ~low, score)) for hit in (hit_first, hit_second)]
    sub = lax.broadcasted_iota(jnp.int32, (tok, tok), 0)
    diagonal = lax.broadcasted_iota(jnp.int32, (tok, tok), 1)
    for k, out in enumerate(outs):
        spread = jnp.where(sub == diagonal, jnp.broadcast_to(out, (tok, tok)), 0.0)
        routing_ref[k : k + 1, :] = jnp.sum(spread, axis=0, keepdims=True)


def joined32(lanes):
    lane = lax.broadcasted_iota(jnp.int32, lanes.shape, 1)
    return jnp.sum(jnp.where(lane < 2, lanes, 0.0), axis=1, keepdims=True)


def outer_kernel(tile, depth, count, *refs):
    lefts, rights, outs = refs[:count], refs[count : 2 * count], refs[2 * count : 3 * count]
    buffer, sems = refs[3 * count :]
    steps = []
    for left, right, out in zip(lefts, rights, outs):
        rows, columns = out.shape
        steps += [(left, right, out, start) for start in range(0, rows, tile)]
    copies = []
    for i, (left, right, out, start) in enumerate(steps):
        slot = i % depth
        if i >= depth:
            copies[i - depth].wait()
        columns = out.shape[1]
        place = buffer.at[slot, :, pl.ds(0, columns)]
        place[...] = dot(left[:, start : start + tile], right[...], 0, 0).astype(BF)
        copies.append(pltpu.make_async_copy(place, out.at[pl.ds(start, tile)], sems.at[slot]))
        copies[i].start()
    for copy in copies[max(0, len(copies) - depth) :]:
        copy.wait()


def outer(pairs, name):
    shapes = [(left.shape[1], right.shape[1]) for left, right in pairs]
    tile = min([512] + [rows for rows, _ in shapes])
    tile = next(size for size in (tile, 384, 256, 128) if all(rows % size == 0 for rows, _ in shapes))
    slots = pairs[0][0].shape[0]
    depth = 4
    widest = max(columns for _, columns in shapes)
    size = sum(rows * columns for rows, columns in shapes)
    return pl.pallas_call(
        functools.partial(outer_kernel, tile, depth, len(pairs)),
        out_shape=[jax.ShapeDtypeStruct(shape, BF) for shape in shapes],
        in_specs=[VMEM] * (2 * len(pairs)),
        out_specs=[ANY] * len(pairs),
        scratch_shapes=[pltpu.VMEM((depth, tile, widest), BF), pltpu.SemaphoreType.DMA((depth,))],
        compiler_params=params(20),
        cost_estimate=cost(8 * slots * size, 2 * size),
        name=name,
    )(*[left for left, _ in pairs], *[right for _, right in pairs])


def shards(n_wide, n_tensor, tokens, cotangent, gates, experts, w_gate, w_up, w_down):
    axes = ("tensor", "wide")
    replicas = n_wide // E
    wide, tensor = lax.axis_index("wide"), lax.axis_index("tensor")
    tok, width = tokens.shape
    hidden = w_gate.shape[2]
    full = 2 * width + LANES
    slots = n_wide * CAP
    position = jnp.stack([tensor, wide // replicas, wide]).astype(jnp.int32)
    expert = (wide // replicas).astype(jnp.int32)[None]

    def swap(value, wide_mask, tensor_mask):
        pairs = [
            (t * n_wide + w, (t ^ tensor_mask) * n_wide + (w ^ wide_mask))
            for t in range(n_tensor)
            for w in range(n_wide)
        ]
        return lax.ppermute(value, axes, pairs)

    def shape(rows, columns, dtype=BF):
        return jax.ShapeDtypeStruct((rows, columns), dtype)

    experts_t = experts.T
    own = (0,)
    rest = tuple(range(1, n_tensor))
    gathered = pl.pallas_call(
        pack_kernel,
        out_shape=pltpu.VMEM((tok, full), BF),
        in_specs=[VMEM] * 4,
        out_specs=VMEM,
        compiler_params=params(2),
        name="pack",
    )(tokens, cotangent, gates.T, experts_t)

    plan = [(w_gate[0], own), (w_up[0], own), (w_gate[0], rest), (w_up[0], rest)]
    staged = []
    offsets = [0]
    mask = n_wide // 2
    while mask >= replicas:
        last = mask == replicas
        got = swap(gathered, mask, 0)
        tokens_done = []
        for weight, which in plan[len(staged) : len(plan) if last else len(staged) + 1]:
            kept_weight, token = stage(position, weight, which, width, gathered)
            staged.append(kept_weight)
            tokens_done.append(token)
        if not last:
            gathered = pl.pallas_call(
                join_kernel,
                out_shape=pltpu.VMEM((2 * gathered.shape[0], full), BF),
                in_specs=[VMEM] * 2 + [ANY] * len(tokens_done),
                out_specs=VMEM,
                compiler_params=params(4),
        name="join",
            )(gathered, got, *tokens_done)
        offsets = offsets + [offset ^ mask for offset in offsets]
        mask //= 2

    chosen = pl.pallas_call(
        select_kernel,
        out_shape=pltpu.VMEM((slots // replicas, full), BF),
        in_specs=[SMEM, VMEM, VMEM] + [ANY] * len(tokens_done),
        out_specs=VMEM,
        compiler_params=params(6),
        name="select",
    )(expert, gathered, got, *tokens_done)
    wg_own, wu_own, wg_rest, wu_rest = staged
    away = [swap(chosen, 0, m) for m in rest]
    near = [chosen] + [swap(chosen, r, 0) for r in range(1, replicas)]

    tiles = max(1, hidden // 512)
    others = n_tensor - 1
    down = pltpu.with_memory_space_constraint(w_down[0], pltpu.HBM)
    partial = pl.pallas_call(
        functools.partial(first_kernel, replicas),
        out_shape=[shape(slots, hidden, F32)] * 3,
        in_specs=[SMEM] + [VMEM] * (replicas + 2) + [ANY],
        out_specs=[VMEM] * 3,
        scratch_shapes=[pltpu.VMEM((1, hidden, width), BF), pltpu.SemaphoreType.DMA((1, tiles))],
        compiler_params=params(16),
        cost_estimate=cost(24 * slots * width * hidden, 6 * width * hidden),
        name="first",
    )(position, *near, wg_own, wu_own, down)

    parts = [[part] + [swap(part, r, 0) for r in range(1, replicas)] for part in away]
    weighted, grad_gate, grad_up, inputs, upstream, score = pl.pallas_call(
        functools.partial(second_kernel, replicas, others),
        out_shape=[shape(slots, hidden)] * 3
        + [shape(slots, width * n_tensor)] * 2
        + [shape(slots, 1, F32)],
        in_specs=[SMEM] + [VMEM] * (replicas * n_tensor + 2) + [ANY] + [VMEM] * 3,
        out_specs=[VMEM] * 6,
        scratch_shapes=[pltpu.VMEM((others, hidden, width), BF), pltpu.SemaphoreType.DMA((others, tiles))],
        compiler_params=params(16),
        cost_estimate=cost(24 * slots * width * hidden, 6 * width * hidden),
        name="second",
    )(position, *near, *sum(parts, []), wg_rest, wu_rest, down, *partial)

    sent = pl.pallas_call(
        functools.partial(back_other_kernel, others),
        out_shape=[shape(slots, width + LANES)] * others,
        in_specs=[VMEM] * 5,
        out_specs=[VMEM] * others,
        compiler_params=params(12),
        cost_estimate=cost(16 * slots * width * hidden, 4 * width * hidden),
        name="back_other",
    )(grad_gate, grad_up, wg_rest, wu_rest, score)
    returned = [swap(value, 0, m) for m, value in zip(rest, sent)]
    kept = pl.pallas_call(
        back_kernel,
        out_shape=shape(slots, width, F32),
        in_specs=[VMEM] * 5,
        out_specs=VMEM,
        compiler_params=params(12),
        cost_estimate=cost(16 * slots * width * hidden, 4 * width * hidden),
        name="back_own",
    )(grad_gate, grad_up, wg_own, wu_own, score)
    (gate_proj_grad,) = outer([(inputs, grad_gate)], "gate_grad")
    half = (width + 2 * LANES) // 2
    merged = pl.pallas_call(
        functools.partial(merge_kernel, replicas, offsets),
        out_shape=shape(2 * slots, half),
        in_specs=[SMEM] + [VMEM] * (2 + others),
        out_specs=VMEM,
        compiler_params=params(8),
        name="merge",
    )(position, kept, score, *returned)
    landed = lax.all_to_all(merged, "wide", split_axis=0, concat_axis=0, tiled=True)
    up_proj_grad, down_proj_grad = outer([(inputs, grad_up), (weighted, upstream)], "other_grads")
    input_grad, routing_grad = pl.pallas_call(
        functools.partial(finish_kernel, replicas),
        out_shape=[shape(tok, width), shape(2, tok, F32)],
        in_specs=[VMEM] * 2,
        out_specs=[VMEM] * 2,
        compiler_params=params(8),
        name="finish",
    )(landed, experts_t)
    return (
        input_grad,
        routing_grad.T,
        gate_proj_grad[None],
        up_proj_grad[None],
        down_proj_grad[None],
    )


def solution(mesh):
    return jax.shard_map(
        functools.partial(shards, mesh.shape["wide"], mesh.shape["tensor"]),
        mesh=mesh,
        in_specs=(
            P("wide", "tensor"),
            P("wide", "tensor"),
            P("wide", None),
            P("wide", None),
            P("wide", None, "tensor"),
            P("wide", None, "tensor"),
            P("wide", "tensor", None),
        ),
        out_specs=(
            P("wide", "tensor"),
            P("wide", None),
            P("wide", None, "tensor"),
            P("wide", None, "tensor"),
            P("wide", "tensor", None),
        ),
        check_vma=False,
    )
```

time: 141 us -> 76.3 us (0.54)
  matrix products: 56.2 us -> 0 us
  Pallas kernels: 0 us -> 50.8 us
  waiting for transfers between devices: 24.4 us -> 6.94 us
  blocking collectives: 15.3 us -> 0 us
  between operations: 14.2 us -> 0.8 us
  starting transfers between devices: 21.6 us -> 14.3 us
  local copies, waits for them, and re-layouts: 5.91 us -> 2.81 us
  other arithmetic: 2.99 us -> 0.08 us
    dot_general x11 -> x0, matrix products: 56.2 us -> none  [the longest x3 25.6 us: contract_cols(): lax.dot_general(left_side, right_side, (((1,), (1,)), ((), ())), preferre...]
    pallas_call x0 -> x16, Pallas kernels: none -> 50.8 us  [the longest x2 14.9 us: outer(): pl.pallas_call(functools.partial(outer_kernel, tile, depth, len(pairs)),...]
    all_to_all x5 -> x1, waiting for transfers between devices: 19.7 us -> 0.01 us  [shards(): lax.all_to_all(merged, 'wide', split_axis=0, concat_axis=0, tiled=True)]
    all_to_all x5 -> x1, starting transfers between devices: 21.6 us -> 3.9 us  [shards(): lax.all_to_all(merged, 'wide', split_axis=0, concat_axis=0, tiled=True)]
    ppermute x0 -> x7, starting transfers between devices: none -> 10.4 us  [swap(): return lax.ppermute(value, axes, pairs)]
    all_gather x2 -> x0, blocking collectives: 10.4 us -> none  [the longest x1 5.66 us: shards(): lax.all_gather(tokens, 'tensor', axis=1, tiled=True)]
    ppermute x0 -> x7, waiting for transfers between devices: none -> 6.94 us  [swap(): return lax.ppermute(value, axes, pairs)]
    psum x1 -> x0, blocking collectives: 4.95 us -> none  [shards(): gate_terms = lax.psum(jnp.sum(through * hidden, axis=1), 'tensor')]
  transfers between devices with their start and end apart: 6 -> 8, of which waited for: 5 -> 2; matrix products, arithmetic and copies ran while one was open for 22% -> 0% of each run, Pallas kernels for 0% -> 50%
where the time goes in v1:
time: 76.3 us; the launch traced here: 75.8 us
  Pallas kernels  50.8 us (67%)
  starting transfers between devices  14.3 us (19%)
  waiting for transfers between devices  6.94 us (9%)
  local copies, waits for them, and re-layouts  2.81 us (4%)
  between operations  0.8 us (1%)
    pallas_call x2, Pallas kernels, outer(): pl.pallas_call(functools.partial(outer_kernel, tile, depth, len(pairs)),...  14.9 us
    pallas_call x4, Pallas kernels, stage(): pl.pallas_call(functools.partial(stage_kernel, parts), out_shape=[pltpu.V...  13.4 us
    ppermute x7, starting transfers between devices, swap(): return lax.ppermute(value, axes, pairs)  10.4 us
    ppermute x7, waiting for transfers between devices, swap(): return lax.ppermute(value, axes, pairs)  6.94 us
    pallas_call x1, Pallas kernels, shards(): pl.pallas_call(functools.partial(second_kernel, replicas, others), out_sh...  6.28 us
    pallas_call x1, Pallas kernels, shards(): pl.pallas_call(functools.partial(first_kernel, replicas), out_shape=[shap...  6.01 us
    all_to_all x1, starting transfers between devices, shards(): lax.all_to_all(merged, 'wide', split_axis=0, concat_axis=0, tiled=True)  3.9 us
    pallas_call x1, Pallas kernels, shards(): pl.pallas_call(back_kernel, out_shape=shape(slots, width, F32), in_specs=...  3.73 us
  transfers between devices with their start and end apart: 8, of which 2 were waited for; matrix products, arithmetic and copies ran while one was open for 0% of the time, Pallas kernels for 50%

profile of v1, /device:TPU:0, one launch (start us, length us, event | category | flops | bytes accessed | tf_op | source)
XLA Modules:
  0.0 75.8 jit_solution(12619304381686150761)
XLA Ops:
  0.6 0.7 copy-done
  1.4 0.7 copy-done.1
  2.1 0.7 copy-done.2
  2.8 0.7 copy-done.4
  3.4 0.1 pack.1.after_ref.own_ref
  3.5 4.1 %collective-permute-start = (bf16[8,3200]{1,0:T(8,128)(2,1)S(1)}, bf16[8,3200]{1,0:T(8,128)(2,1)S(1)}, u32[]{:S(2)}, u32[]{:S(2)}) collective-permute-start(bf16[8,3200]{1,0:T(8,128)(2,1)S(1)} %pack.1.after_ref.own_ref), channel_id=1, source_target_pairs={{0,8},{1,9},{2,10},{3,11},{4,12},{5,13},{6,14},{7,15},{8,0},{9,1},... | collective-permute-start | bytes 153608 | tf_op jit(solution)/shard_map/ppermute | solution.py:355
  7.6 0.1 pad_add_fusion.position_ref
  7.7 3.3 %stage.4 = (bf16[1536,2048]{1,0:T(8,128)(2,1)S(1)}, f32[8,128]{1,0:T(8,128)S(1)}) custom-call(s32[3]{0:T(128)S(1)} %pad_add_fusion.position_ref, bf16[8,3200]{1,0:T(8,128)(2,1)S(1)} %pack.1.after_ref.own_ref, bf16[3072,2048]{1,0:T(8,128)(2,1)} %bitcast.22), custom_call_target="tpu_custom_call" | custom-call | bytes 12582912 | tf_op jit(solution)/shard_map/stage/pallas_call | solution.py:90
  11.1 0.0 collective-permute-done.got_ref
  11.1 1.6 %collective-permute-start.1 = (bf16[16,3200]{1,0:T(8,128)(2,1)S(1)}, bf16[16,3200]{1,0:T(8,128)(2,1)S(1)}, u32[]{:S(2)}, u32[]{:S(2)}) collective-permute-start(bf16[16,3200]{1,0:T(8,128)(2,1)S(1)} %join.2.after_ref.own_ref), channel_id=1, source_target_pairs={{0,4},{1,5},{2,6},{3,7},{4,0},{5,1},{6,2},{7,3},{8,12},{9,13},{10,... | collective-permute-start | bytes 307208 | tf_op jit(solution)/shard_map/ppermute | solution.py:355
  12.7 3.3 %stage.5 = (bf16[1536,2048]{1,0:T(8,128)(2,1)S(1)}, f32[8,128]{1,0:T(8,128)S(1)}) custom-call(s32[3]{0:T(128)S(1)} %pad_add_fusion.position_ref, bf16[16,3200]{1,0:T(8,128)(2,1)S(1)} %join.2.after_ref.own_ref, bf16[3072,2048]{1,0:T(8,128)(2,1)} %bitcast.18), custom_call_target="tpu_custom_call" | custom-call | bytes 12582912 | tf_op jit(solution)/shard_map/stage/pallas_call | solution.py:90
  16.1 1.6 %collective-permute-start.2 = (bf16[32,3200]{1,0:T(8,128)(2,1)S(1)}, bf16[32,3200]{1,0:T(8,128)(2,1)S(1)}, u32[]{:S(2)}, u32[]{:S(2)}) collective-permute-start(bf16[32,3200]{1,0:T(8,128)(2,1)S(1)} %join.3.after_ref.own_ref), channel_id=1, source_target_pairs={{0,2},{1,3},{2,0},{3,1},{4,6},{5,7},{6,4},{7,5},{8,10},{9,11},{10,... | collective-permute-start | bytes 614408 | tf_op jit(solution)/shard_map/ppermute | solution.py:355
  17.7 3.4 %stage.7 = (bf16[1536,2048]{1,0:T(8,128)(2,1)S(1)}, f32[8,128]{1,0:T(8,128)S(1)}) custom-call(s32[3]{0:T(128)S(1)} %pad_add_fusion.position_ref, bf16[32,3200]{1,0:T(8,128)(2,1)S(1)} %join.3.after_ref.own_ref, bf16[3072,2048]{1,0:T(8,128)(2,1)} %bitcast.19), custom_call_target="tpu_custom_call" | custom-call | bytes 12582912 | tf_op jit(solution)/shard_map/stage/pallas_call | solution.py:90
  21.1 3.3 %stage.6 = (bf16[1536,2048]{1,0:T(8,128)(2,1)S(1)}, f32[8,128]{1,0:T(8,128)S(1)}) custom-call(s32[3]{0:T(128)S(1)} %pad_add_fusion.position_ref, bf16[32,3200]{1,0:T(8,128)(2,1)S(1)} %join.3.after_ref.own_ref, bf16[3072,2048]{1,0:T(8,128)(2,1)} %bitcast.23), custom_call_target="tpu_custom_call" | custom-call | bytes 12582912 | tf_op jit(solution)/shard_map/stage/pallas_call | solution.py:90
  24.4 0.0 collective-permute-done.2.got_ref
  24.4 0.4 select.5.refs_0_
  24.8 1.6 %collective-permute-start.4 = (bf16[32,3200]{1,0:T(8,128)(2,1)S(1)}, bf16[32,3200]{1,0:T(8,128)(2,1)S(1)}, u32[]{:S(2)}, u32[]{:S(2)}) collective-permute-start(bf16[32,3200]{1,0:T(8,128)(2,1)S(1)} %select.5.refs_0_), channel_id=1, source_target_pairs={{0,16},{1,17},{2,18},{3,19},{4,20},{5,21},{6,22},{7,23},{8,24},{9,... | collective-permute-start | bytes 614408 | tf_op jit(solution)/shard_map/ppermute | solution.py:355
  26.4 0.0 collective-permute-start.3
  26.4 4.5 %collective-permute-done.4.refs_2_ = bf16[32,3200]{1,0:T(8,128)(2,1)S(1)} collective-permute-done((bf16[32,3200]{1,0:T(8,128)(2,1)S(1)}, bf16[32,3200]{1,0:T(8,128)(2,1)S(1)}, u32[]{:S(2)}, u32[]{:S(2)}) %collective-permute-start.4) | collective-permute-done | bytes 204832 | tf_op jit(solution)/shard_map/ppermute | solution.py:355
  30.8 6.0 %first.1 = (f32[64,2048]{1,0:T(8,128)S(1)}, f32[64,2048]{1,0:T(8,128)S(1)}, f32[64,2048]{1,0:T(8,128)S(1)}) custom-call(s32[3]{0:T(128)S(1)} %pad_add_fusion.position_ref, bf16[32,3200]{1,0:T(8,128)(2,1)S(1)} %select.5.refs_0_, bf16[32,3200]{1,0:T(8,128)(2,1)S(1)} %collective-permute-done.3.refs_1_, bf16[1536,2048]{1,0:T(8,128)(2,1)S(1)} %get-tuple-element.32.refs_2_.w_gate, ...), custom_call_target="tpu_custom_call" | custom-call | flops 4831838208 | bytes 18874368 | tf_op jit(solution)/shard_map/first/pallas_call | solution.py:411
  36.9 6.3 %second.1 = (bf16[64,2048]{1,0:T(8,128)(2,1)S(1)}, bf16[64,2048]{1,0:T(8,128)(2,1)S(1)}, bf16[64,2048]{1,0:T(8,128)(2,1)S(1)}, bf16[64,3072]{1,0:T(8,128)(2,1)S(...) custom-call(s32[3]{0:T(128)S(1)} %pad_add_fusion.position_ref, bf16[32,3200]{1,0:T(8,128)(2,1)S(1)} %select.5.refs_0_, ...), custom_call_target="tpu_custom_call" | custom-call | flops 4831838208 | bytes 18874368 | tf_op jit(solution)/shard_map/second/pallas_call | solution.py:423
  43.2 3.5 %back_other.1 = bf16[64,1664]{1,0:T(8,128)(2,1)S(1)} custom-call(bf16[64,2048]{1,0:T(8,128)(2,1)S(1)} %get-tuple-element.37.grad_gate.refs_0_.refs_1_, bf16[64,2048]{1,0:T(8,128)(2,1)S(1)} %get-tuple-element.38.grad_up.refs_1_.refs_2_, bf16[1536,2048]{1,0:T(8,128)(2,1)S(1)} %get-tuple-element.30.refs_4_.refs_2_, ...), custom_call_target="tpu_custom_call" | custom-call | flops 3221225472 | bytes 12582912 | tf_op jit(solution)/shard_map/back_other/pallas_call | solution.py:436
  46.7 1.6 %collective-permute-start.6 = (bf16[64,1664]{1,0:T(8,128)(2,1)S(1)}, bf16[64,1664]{1,0:T(8,128)(2,1)S(1)}, u32[]{:S(2)}, u32[]{:S(2)}) collective-permute-start(bf16[64,1664]{1,0:T(8,128)(2,1)S(1)} %back_other.1), channel_id=1, source_target_pairs={{0,16},{1,17},{2,18},{3,19},{4,20},{5,21},{6,22},{7,23},{8,24},{9,... | collective-permute-start | bytes 638984 | tf_op jit(solution)/shard_map/ppermute | solution.py:355
  48.2 3.7 %back_own.1.own_ref = f32[64,1536]{1,0:T(8,128)S(1)} custom-call(bf16[64,2048]{1,0:T(8,128)(2,1)S(1)} %get-tuple-element.37.grad_gate.refs_0_.refs_1_, bf16[64,2048]{1,0:T(8,128)(2,1)S(1)} %get-tuple-element.38.grad_up.refs_1_.refs_2_, bf16[1536,2048]{1,0:T(8,128)(2,1)S(1)} %get-tuple-element.32.refs_2_.w_gate, ...), custom_call_target="tpu_custom_call" | custom-call | flops 3221225472 | bytes 12582912 | tf_op jit(solution)/shard_map/back_own/pallas_call | solution.py:446
  52.0 2.4 %collective-permute-done.6.refs_0_ = bf16[64,1664]{1,0:T(8,128)(2,1)S(1)} collective-permute-done((bf16[64,1664]{1,0:T(8,128)(2,1)S(1)}, bf16[64,1664]{1,0:T(8,128)(2,1)S(1)}, u32[]{:S(2)}, u32[]{:S(2)}) %collective-permute-start.6) | collective-permute-done | bytes 213024 | tf_op jit(solution)/shard_map/ppermute | solution.py:355
  54.4 1.6 %merge.1 = bf16[128,896]{1,0:T(8,128)(2,1)} custom-call(s32[3]{0:T(128)S(1)} %pad_add_fusion.position_ref, f32[64,1536]{1,0:T(8,128)S(1)} %back_own.1.own_ref, f32[64,1]{1,0:T(8,128)S(1)} %get-tuple-element.39.routing_ref.refs_4_, bf16[64,1664]{1,0:T(8,128)(2,1)S(1)} %collective-permute-done.6.refs_0_), custom_call_target="tpu_custom_call" | custom-call | tf_op jit(solution)/shard_map/merge/pallas_call | solution.py:457
  56.0 3.9 %all-to-all-start = ((bf16[16,8,896]{2,1,0:T(8,128)(2,1)}), bf16[16,8,896]{2,1,0:T(8,128)(2,1)S(1)}, u32[]{:S(2)}, u32[]{:S(2)}) async-start(bf16[16,8,896]{2,1,0:T(8,128)(2,1)} %bitcast.8), calls=%async_computation | async-start | bytes 458752 | tf_op jit(solution)/shard_map/all_to_all | solution.py:465
  59.9 0.0 copy-start.3
  59.9 9.5 %other_grads.1 = (bf16[3072,2048]{1,0:T(8,128)(2,1)}, bf16[2048,3072]{1,0:T(8,128)(2,1)}) custom-call(bf16[64,3072]{1,0:T(8,128)(2,1)S(1)} %get-tuple-element.42.refs_0_, bf16[64,2048]{1,0:T(8,128)(2,1)S(1)} %get-tuple-element.43.refs_1_, bf16[64,2048]{1,0:T(8,128)(2,1)S(1)} %get-tuple-element.38.grad_up.refs_1_.refs_2_, ...), custom_call_target="tpu_custom_call" | custom-call | flops 6442450944 | bytes 25165824 | tf_op jit(solution)/shard_map/other_grads/pallas_call | solution.py:326
  69.5 5.4 %gate_grad.1 = bf16[3072,2048]{1,0:T(8,128)(2,1)} custom-call(bf16[64,3072]{1,0:T(8,128)(2,1)S(1)} %get-tuple-element.42.refs_0_, bf16[64,2048]{1,0:T(8,128)(2,1)S(1)} %get-tuple-element.37.grad_gate.refs_0_.refs_1_), custom_call_target="tpu_custom_call" | custom-call | flops 3221225472 | bytes 12582912 | tf_op jit(solution)/shard_map/gate_grad/pallas_call | solution.py:326
  74.9 0.0 all-to-all-done
  74.9 0.9 %finish.1 = (bf16[8,1536]{1,0:T(8,128)(2,1)}, f32[2,8]{1,0:T(2,128)}) custom-call(bf16[128,896]{1,0:T(8,128)(2,1)S(1)} %bitcast.14, s32[2,8]{1,0:T(2,128)S(1)} %bitcast.16), custom_call_target="tpu_custom_call" | custom-call | tf_op jit(solution)/shard_map/finish/pallas_call | solution.py:467
  (11 shorter events, 0.0 us)
Async XLA Ops:
  0.6 0.7 copy-start
  1.4 0.7 copy-start.1
  2.1 0.7 copy-start.2
  2.8 0.7 copy-start.4
  3.5 7.5 %collective-permute-start = (bf16[8,3200]{1,0:T(8,128)(2,1)S(1)}, bf16[8,3200]{1,0:T(8,128)(2,1)S(1)}, u32[]{:S(2)}, u32[]{:S(2)}) collective-permute-start(bf16[8,3200]{1,0:T(8,128)(2,1)S(1)} %pack.1.after_ref.own_ref), channel_id=1, source_target_pairs={{0,8},{1,9},{2,10},{3,11},{4,12},{5,13},{6,14},{7,15},{8,0},{9,1},... | collective-permute-start | bytes 153608 | tf_op jit(solution)/shard_map/ppermute | solution.py:355
  11.1 5.0 %collective-permute-start.1 = (bf16[16,3200]{1,0:T(8,128)(2,1)S(1)}, bf16[16,3200]{1,0:T(8,128)(2,1)S(1)}, u32[]{:S(2)}, u32[]{:S(2)}) collective-permute-start(bf16[16,3200]{1,0:T(8,128)(2,1)S(1)} %join.2.after_ref.own_ref), channel_id=1, source_target_pairs={{0,4},{1,5},{2,6},{3,7},{4,0},{5,1},{6,2},{7,3},{8,12},{9,13},{10,... | collective-permute-start | bytes 307208 | tf_op jit(solution)/shard_map/ppermute | solution.py:355
  16.1 8.3 %collective-permute-start.2 = (bf16[32,3200]{1,0:T(8,128)(2,1)S(1)}, bf16[32,3200]{1,0:T(8,128)(2,1)S(1)}, u32[]{:S(2)}, u32[]{:S(2)}) collective-permute-start(bf16[32,3200]{1,0:T(8,128)(2,1)S(1)} %join.3.after_ref.own_ref), channel_id=1, source_target_pairs={{0,2},{1,3},{2,0},{3,1},{4,6},{5,7},{6,4},{7,5},{8,10},{9,11},{10,... | collective-permute-start | bytes 614408 | tf_op jit(solution)/shard_map/ppermute | solution.py:355
  24.8 6.0 %collective-permute-start.4 = (bf16[32,3200]{1,0:T(8,128)(2,1)S(1)}, bf16[32,3200]{1,0:T(8,128)(2,1)S(1)}, u32[]{:S(2)}, u32[]{:S(2)}) collective-permute-start(bf16[32,3200]{1,0:T(8,128)(2,1)S(1)} %select.5.refs_0_), channel_id=1, source_target_pairs={{0,16},{1,17},{2,18},{3,19},{4,20},{5,21},{6,22},{7,23},{8,24},{9,... | collective-permute-start | bytes 614408 | tf_op jit(solution)/shard_map/ppermute | solution.py:355
  26.4 4.5 %collective-permute-start.3 = (bf16[32,3200]{1,0:T(8,128)(2,1)S(1)}, bf16[32,3200]{1,0:T(8,128)(2,1)S(1)}, u32[]{:S(2)}, u32[]{:S(2)}) collective-permute-start(bf16[32,3200]{1,0:T(8,128)(2,1)S(1)} %select.5.refs_0_), channel_id=1, source_target_pairs={{0,1},{1,0},{2,3},{3,2},{4,5},{5,4},{6,7},{7,6},{8,9},{9,8},{10,11... | collective-permute-start | bytes 614408 | tf_op jit(solution)/shard_map/ppermute | solution.py:355
  30.8 6.0 %collective-permute-start.5 = (bf16[32,3200]{1,0:T(8,128)(2,1)S(1)}, bf16[32,3200]{1,0:T(8,128)(2,1)S(1)}, u32[]{:S(2)}, u32[]{:S(2)}) collective-permute-start(bf16[32,3200]{1,0:T(8,128)(2,1)S(1)} %collective-permute-done.4.refs_2_), channel_id=1, source_target_pairs={{0,1},{1,0},{2,3},{3,2},{4,5},{5,4},{6,7},{7,6},{8,9},{9,8},{10,11... | collective-permute-start | bytes 614408 | tf_op jit(solution)/shard_map/ppermute | solution.py:355
  46.7 7.7 %collective-permute-start.6 = (bf16[64,1664]{1,0:T(8,128)(2,1)S(1)}, bf16[64,1664]{1,0:T(8,128)(2,1)S(1)}, u32[]{:S(2)}, u32[]{:S(2)}) collective-permute-start(bf16[64,1664]{1,0:T(8,128)(2,1)S(1)} %back_other.1), channel_id=1, source_target_pairs={{0,16},{1,17},{2,18},{3,19},{4,20},{5,21},{6,22},{7,23},{8,24},{9,... | collective-permute-start | bytes 638984 | tf_op jit(solution)/shard_map/ppermute | solution.py:355
  56.0 18.8 %all-to-all-start = ((bf16[16,8,896]{2,1,0:T(8,128)(2,1)}), bf16[16,8,896]{2,1,0:T(8,128)(2,1)S(1)}, u32[]{:S(2)}, u32[]{:S(2)}) async-start(bf16[16,8,896]{2,1,0:T(8,128)(2,1)} %bitcast.8), calls=%async_computation | async-start | bytes 458752 | tf_op jit(solution)/shard_map/all_to_all | solution.py:465
  59.9 14.9 %copy-start.3 = (s32[8,2]{0,1:T(2,128)S(1)}, s32[8,2]{0,1:T(2,128)}, u32[]{:S(2)}) copy-start(s32[8,2]{0,1:T(2,128)} %param.10) | copy-start | bytes 196

commit v2 on v1

v2 whole, which is shorter than its diff:
```python
import functools

import jax
import jax.numpy as jnp
from jax import lax
from jax.experimental import pallas as pl
from jax.experimental.pallas import tpu as pltpu
from jax.sharding import PartitionSpec as P

E = 8
CAP = 4
LANES = 128
BF = jnp.bfloat16
F32 = jnp.float32
VMEM = pl.BlockSpec(memory_space=pltpu.VMEM)
SMEM = pl.BlockSpec(memory_space=pltpu.SMEM)
ANY = pl.BlockSpec(memory_space=pl.ANY)


def dot(left, right, left_dim, right_dim):
    return lax.dot_general(
        left, right, (((left_dim,), (right_dim,)), ((), ())), preferred_element_type=F32
    )


def params(mib):
    return pltpu.CompilerParams(vmem_limit_bytes=mib << 20)


def cost(flops, moved):
    return pl.CostEstimate(flops=flops, bytes_accessed=moved, transcendentals=0)


def column(row):
    n = row.shape[1]
    sub = lax.broadcasted_iota(jnp.int32, (n, n), 0)
    lane = lax.broadcasted_iota(jnp.int32, (n, n), 1)
    return jnp.sum(jnp.where(sub == lane, jnp.broadcast_to(row, (n, n)), 0.0), axis=1, keepdims=True)


def routing(experts_ref, lane_expert):
    ids = experts_ref[...].astype(F32)
    first, second = column(ids[0:1, :]), column(ids[1:2, :])
    hit_first = lane_expert == first
    hit_second = lane_expert == second
    picked = jnp.where(hit_first | hit_second, 1.0, 0.0)
    sub = lax.broadcasted_iota(jnp.int32, picked.shape, 0)
    before = jnp.zeros_like(picked)
    for row in range(picked.shape[0] - 1):
        before = before + jnp.where(sub > row, picked[row : row + 1, :], 0.0)
    return hit_first, hit_second, picked, before


def pack_kernel(
    tokens_hbm, cotangent_hbm, gates_hbm, experts_hbm, out_ref, gates_ref, experts_ref, sems
):
    rows, width = tokens_hbm.shape
    copies = [
        pltpu.make_async_copy(source, target, sems.at[i])
        for i, (source, target) in enumerate(
            (
                (gates_hbm, gates_ref),
                (experts_hbm, experts_ref),
                (tokens_hbm, out_ref.at[:, pl.ds(0, width)]),
                (cotangent_hbm, out_ref.at[:, pl.ds(width, width)]),
            )
        )
    ]
    for copy in copies:
        copy.start()
    copies[0].wait()
    copies[1].wait()
    lane = lax.broadcasted_iota(jnp.int32, (rows, LANES), 1)
    lane_expert = (lane % E).astype(F32)
    hit_first, hit_second, picked, before = routing(experts_ref, lane_expert)
    gates = gates_ref[...].astype(F32)
    gate = jnp.where(hit_first, column(gates[0:1, :]), 0.0) + jnp.where(
        hit_second, column(gates[1:2, :]), 0.0
    )
    place = jnp.where(picked > 0.5, before, -1.0)
    info = jnp.where(lane < E, place, jnp.where(lane < 2 * E, gate, 0.0))
    out_ref[:, 2 * width :] = info.astype(BF)
    copies[2].wait()
    copies[3].wait()


def part_copies(position, by_row, masks, source, target, sems):
    copies = []
    for i, mask in enumerate(masks):
        if by_row:
            width = target.shape[0] // len(masks)
            place = pl.ds(pl.multiple_of((position ^ mask) * width, width), width)
            pair = (source.at[place], target.at[pl.ds(i * width, width)])
        else:
            width = target.shape[1]
            depth = target.shape[0] // len(masks)
            place = pl.ds(pl.multiple_of((position ^ mask) * width, width), width)
            pair = (source.at[:, place], target.at[pl.ds(i * depth, depth)])
        copies.append(pltpu.make_async_copy(*pair, sems.at[i]))
    return copies


def part_shape(weight, by_row, masks, width):
    if by_row:
        return pltpu.VMEM((width * len(masks), weight.shape[1]), BF)
    return pltpu.VMEM((weight.shape[0] * len(masks), width), BF)


def stage_kernel(jobs, position_ref, after_ref, *refs):
    count = len(jobs)
    sources, outs = refs[:count], refs[count : 2 * count]
    token_ref = refs[2 * count]
    copies = []
    for (by_row, masks), source, out, sems in zip(jobs, sources, outs, refs[2 * count + 1 :]):
        copies += part_copies(position_ref[0], by_row, masks, source, out, sems)
    for copy in copies:
        copy.start()
    token_ref[...] = jnp.zeros_like(token_ref)
    for copy in copies:
        copy.wait()


def stage(position, jobs, width, after):
    outs = [part_shape(*job, width) for job in jobs]
    size = sum(out.shape[0] * out.shape[1] for out in outs)
    *kept, token = pl.pallas_call(
        functools.partial(stage_kernel, [job[1:] for job in jobs]),
        out_shape=outs + [pltpu.VMEM((8, LANES), F32)],
        in_specs=[SMEM, ANY] + [ANY] * len(jobs),
        out_specs=[ANY] * len(jobs) + [VMEM],
        scratch_shapes=[pltpu.SemaphoreType.DMA((len(job[2]),)) for job in jobs],
        compiler_params=params(2),
        cost_estimate=cost(0, 4 * size),
        name="stage",
    )(position, after, *[pltpu.with_memory_space_constraint(job[0], pltpu.HBM) for job in jobs])
    return kept, token


def join_kernel(own_ref, got_ref, *refs):
    out_ref = refs[-1]
    rows = own_ref.shape[0]
    out_ref[:rows, :] = own_ref[...]
    out_ref[rows:, :] = got_ref[...]


def relay_kernel(value_ref, *refs):
    refs[-1][...] = value_ref[...]


def relay(value, after):
    return pl.pallas_call(
        relay_kernel,
        out_shape=pltpu.VMEM(value.shape, value.dtype),
        in_specs=[VMEM, ANY],
        out_specs=VMEM,
        compiler_params=params(2),
        name="relay",
    )(value, after)


def select_kernel(expert_ref, source_ref, *refs):
    out_ref = refs[-1]
    tok_rows, full = source_ref.shape
    slots = out_ref.shape[0]
    per_block = tok_rows // (slots // CAP)
    info = source_ref[:, full - LANES :].astype(F32)
    lane = lax.broadcasted_iota(jnp.int32, info.shape, 1)
    place = jnp.sum(jnp.where(lane == expert_ref[0], info, 0.0), axis=1, keepdims=True)
    row = lax.broadcasted_iota(jnp.int32, (tok_rows, slots), 0)
    col = lax.broadcasted_iota(jnp.int32, (tok_rows, slots), 1)
    take = (row // per_block == col // CAP) & (place == (col % CAP).astype(F32))
    out_ref[...] = dot(jnp.where(take, 1.0, 0.0).astype(BF), source_ref[...], 0, 0).astype(BF)


def select(expert, source, blocks, after):
    return pl.pallas_call(
        select_kernel,
        out_shape=pltpu.VMEM((blocks * CAP, source.shape[1]), BF),
        in_specs=[SMEM, VMEM, ANY],
        out_specs=VMEM,
        compiler_params=params(4),
        name="select",
    )(expert, source, after)


def stacked(refs, start, size):
    return jnp.concatenate([ref[:, start : start + size] for ref in refs], axis=0)


def low_high(rows):
    zeros = jnp.zeros_like(rows)
    return jnp.concatenate([rows, zeros], axis=0), jnp.concatenate([zeros, rows], axis=0)


def folded(weight, low, high):
    half = weight.shape[0] // 2
    return dot(weight[:half, :], low, 1, 1) + dot(weight[half:, :], high, 1, 1)


def first_kernel(count, position_ref, *refs):
    parts = refs[:count]
    w_gate, w_up, w_down, gate_out, up_out, through_out = refs[count:]
    width = w_gate.shape[0]
    here = pl.ds(pl.multiple_of(position_ref[0] * width, width), width)
    hidden = w_gate.shape[1]
    tile = min(512, hidden)
    inputs = stacked(parts, 0, width)
    upstream = stacked(parts, width, width)
    through_out[...] = folded(w_down.at[:, here], *low_high(upstream))
    for start in range(0, hidden, tile):
        units = slice(start, start + tile)
        gate_out[:, units] = dot(inputs, w_gate[:, units], 1, 0)
        up_out[:, units] = dot(inputs, w_up[here, units], 1, 0)


def second_kernel(count, others, position_ref, *refs):
    own = refs[:count]
    parts = [refs[count * (m + 1) : count * (m + 2)] for m in range(others)]
    rest = refs[count * (others + 1) :]
    w_gate, w_up, w_down, gate_in, up_in, through_in = rest[:6]
    weighted_ref, grad_gate_ref, grad_up_ref, inputs_ref, upstream_ref, routing_ref = rest[6:12]
    through_ref = rest[12]
    full = own[0].shape[1]
    width = (full - LANES) // 2
    position, expert = position_ref[0], position_ref[1]
    places = [pl.ds(pl.multiple_of((position ^ m) * width, width), width) for m in range(others + 1)]
    hidden = w_gate.shape[1]
    slots = gate_in.shape[0]
    half = hidden // 2
    tile = min(512, half)
    through = through_in[...]
    for m in range(others):
        upstream = stacked(parts[m], width, width)
        through = through + folded(w_down.at[:, places[m + 1]], *low_high(upstream))
    through_ref[...] = through.T
    info = stacked(own, full - LANES, LANES).astype(F32)
    lane = lax.broadcasted_iota(jnp.int32, info.shape, 1)
    scale = jnp.sum(jnp.where(lane == expert + E, info, 0.0), axis=1, keepdims=True)
    for m, blocks in enumerate([own] + parts):
        inputs_ref[:, places[m]] = stacked(blocks, 0, width)
        upstream_ref[:, places[m]] = stacked(blocks, width, width)
    xs = [stacked(part, 0, width) for part in parts]
    x = jnp.concatenate(xs, axis=1)
    score = jnp.zeros((slots, 1), F32)
    for start in range(0, hidden, tile):
        units = slice(start, start + tile)
        pre_gate = gate_in[:, units] + dot(x, w_gate[:, units], 1, 0)
        pre_up = up_in[:, units]
        for m in range(others):
            pre_up = pre_up + dot(xs[m], w_up[places[m + 1], units], 1, 0)
        side, offset = divmod(start, half)
        through = through_ref[side * slots : (side + 1) * slots, offset : offset + tile]
        sig = jax.nn.sigmoid(pre_gate)
        act = pre_gate * sig
        product = act * pre_up
        weighted_ref[:, units] = (scale * product).astype(BF)
        score = score + jnp.sum(through * product, axis=1, keepdims=True)
        scaled = scale * through
        grad_gate_ref[:, units] = (scaled * pre_up * sig * (1.0 + pre_gate * (1.0 - sig))).astype(BF)
        grad_up_ref[:, units] = (scaled * act).astype(BF)
    sub = lax.broadcasted_iota(jnp.int32, (slots, slots), 0)
    diagonal = lax.broadcasted_iota(jnp.int32, (slots, slots), 1)
    spread = jnp.where(sub == diagonal, jnp.broadcast_to(score, (slots, slots)), 0.0)
    routing_ref[...] = jnp.sum(spread, axis=0, keepdims=True)


def halves(row, rows):
    high = row.astype(BF).astype(F32)
    wide = jnp.concatenate([high, row - high], axis=1)
    sub = lax.broadcasted_iota(jnp.int32, (rows, wide.shape[1]), 0)
    return jnp.where(sub == 0, jnp.broadcast_to(wide, sub.shape), 0.0).astype(BF)


def back(position, mask, grad_gate, grad_up, w_gate, w_up, routing_ref, out_ref):
    width = w_gate.shape[0]
    half = width // 2

    def products(rows):
        part = folded(w_gate, *low_high(grad_gate[...])) + folded(w_up.at[rows], *low_high(grad_up[...]))
        out_ref[:half, :] = part.astype(out_ref.dtype)

    places = w_up.shape[0] // width
    if places == 2:
        for place in range(places):
            pl.when(position ^ mask == place)(functools.partial(products, pl.ds(place * width, width)))
    else:
        products(pl.ds(pl.multiple_of((position ^ mask) * width, width), width))
    if out_ref.shape[0] > half:
        out_ref[half:, :] = halves(routing_ref[...], out_ref.shape[0] - half)


def back_own_kernel(position_ref, *refs):
    back(position_ref[0], 0, *refs)


def back_other_kernel(others, position_ref, *refs):
    grad_gate, grad_up, w_gate, w_up, routing_ref = refs[:5]
    outs = refs[5:]
    width = w_gate.shape[0] // others
    for m, out_ref in enumerate(outs):
        rows = pl.ds(m * width, width)
        back(position_ref[0], m + 1, grad_gate, grad_up, w_gate.at[rows], w_up, routing_ref, out_ref)


def merge_kernel(after_ref, order_ref, own_ref, routing_ref, *refs):
    parts, out_ref = refs[:-1], refs[-1]
    half, lanes = own_ref.shape
    slots = lanes // 2
    total = own_ref[...]
    score = routing_ref[...]
    for part in parts:
        total = total + part[:half, :].astype(F32)
        tail = part[half : half + 1, :].astype(F32)
        score = score + tail[:, :slots] + tail[:, slots:]
    columns = jnp.concatenate([total.astype(BF), halves(score, out_ref.shape[1] - half)], axis=0)
    out_ref[...] = dot(order_ref[...], columns, 1, 1).astype(BF)


def plan_kernel(replicas, offsets, position_ref, experts_ref, after_ref, order_ref, *hit_refs):
    size = order_ref.shape[0]
    slots = size // 2
    out_row = lax.broadcasted_iota(jnp.int32, (size, size), 0)
    lane = lax.broadcasted_iota(jnp.int32, (size, size), 1)
    high = lane >= slots
    slot = jnp.where(high, lane - slots, lane)
    block = slot // CAP
    blocks = len(offsets)
    origin = jnp.zeros_like(slot)
    for r in range(replicas):
        for j, offset in enumerate(offsets):
            origin = jnp.where(block == r * blocks + j, offset ^ r, origin)
    origin = origin ^ position_ref[2]
    target = origin * (2 * CAP) + (slot - block * CAP) + jnp.where(high, CAP, 0)
    order_ref[...] = jnp.where(out_row == target, 1.0, 0.0).astype(BF)
    tok = experts_ref.shape[1]
    lane = lax.broadcasted_iota(jnp.int32, (tok, size), 1)
    lane_expert = (lane // (2 * CAP * replicas)).astype(F32)
    hit_first, hit_second, _, before = routing(experts_ref, lane_expert)
    here = before == (lane % CAP).astype(F32)
    low = lane % (2 * CAP) < CAP
    any_hit = (hit_first | hit_second) & here
    for ref, hit in zip(hit_refs, (any_hit & low, any_hit & ~low, hit_first & here, hit_second & here)):
        ref[...] = jnp.where(hit, 1.0, 0.0).astype(BF)


def finish_kernel(back_ref, low_ref, high_ref, first_ref, second_ref, grad_ref, routing_ref):
    tok, width = grad_ref.shape
    half = width // 2
    grad_ref[:, :half] = dot(low_ref[...], back_ref[:, :half], 1, 0).astype(BF)
    grad_ref[:, half:] = dot(high_ref[...], back_ref[:, :half], 1, 0).astype(BF)
    sub = lax.broadcasted_iota(jnp.int32, (tok, tok), 0)
    diagonal = lax.broadcasted_iota(jnp.int32, (tok, tok), 1)
    for k, ref in enumerate((first_ref, second_ref)):
        score = dot(ref[...], back_ref[:, half : half + LANES], 1, 0)[:, :1]
        spread = jnp.where(sub == diagonal, jnp.broadcast_to(score, (tok, tok)), 0.0)
        routing_ref[k : k + 1, :] = jnp.sum(spread, axis=0, keepdims=True)


def outer_kernel(tile, depth, count, *refs):
    lefts, rights, outs = refs[:count], refs[count : 2 * count], refs[2 * count : 3 * count]
    buffer, turned, sems = refs[3 * count :]
    steps = []
    for left, right, out in zip(lefts, rights, outs):
        rows, columns = out.shape
        steps += [(left, right, out, start) for start in range(0, rows, tile)]
    copies = []
    for i, (left, right, out, start) in enumerate(steps):
        slot = i % depth
        if start == 0:
            turned[: out.shape[0], :] = left[...].T
        if i >= depth:
            copies[i - depth].wait()
        columns = out.shape[1]
        place = buffer.at[slot, :, pl.ds(0, columns)]
        place[...] = dot(turned[start : start + tile, :], right[...], 1, 0).astype(BF)
        copies.append(pltpu.make_async_copy(place, out.at[pl.ds(start, tile)], sems.at[slot]))
        copies[i].start()
    for copy in copies[max(0, len(copies) - depth) :]:
        copy.wait()


def outer(pairs, name, weight=1):
    shapes = [(left.shape[1], right.shape[1]) for left, right in pairs]
    tile = min([512] + [rows for rows, _ in shapes])
    tile = next(size for size in (tile, 384, 256, 128) if all(rows % size == 0 for rows, _ in shapes))
    slots = pairs[0][0].shape[0]
    depth = 4
    widest = max(columns for _, columns in shapes)
    tallest = max(rows for rows, _ in shapes)
    size = sum(rows * columns for rows, columns in shapes)
    return pl.pallas_call(
        functools.partial(outer_kernel, tile, depth, len(pairs)),
        out_shape=[jax.ShapeDtypeStruct(shape, BF) for shape in shapes],
        in_specs=[VMEM] * (2 * len(pairs)),
        out_specs=[ANY] * len(pairs),
        scratch_shapes=[
            pltpu.VMEM((depth, tile, widest), BF),
            pltpu.VMEM((tallest, slots), BF),
            pltpu.SemaphoreType.DMA((depth,)),
        ],
        compiler_params=params(20),
        cost_estimate=cost(8 * slots * size // weight, 2 * size // weight),
        name=name,
    )(*[left for left, _ in pairs], *[right for _, right in pairs])


def shards(n_wide, n_tensor, tokens, cotangent, gates, experts, w_gate, w_up, w_down):
    axes = ("tensor", "wide")
    replicas = n_wide // E
    wide, tensor = lax.axis_index("wide"), lax.axis_index("tensor")
    tok, width = tokens.shape
    hidden = w_gate.shape[2]
    full = 2 * width + LANES
    slots = n_wide * CAP
    position = jnp.stack([tensor, wide // replicas, wide]).astype(jnp.int32)
    expert = (wide // replicas).astype(jnp.int32)[None]

    def swap(value, wide_mask, tensor_mask):
        pairs = [
            (t * n_wide + w, (t ^ tensor_mask) * n_wide + (w ^ wide_mask))
            for t in range(n_tensor)
            for w in range(n_wide)
        ]
        return lax.ppermute(value, axes, pairs)

    def shape(rows, columns, dtype=BF):
        return jax.ShapeDtypeStruct((rows, columns), dtype)

    experts_t = experts.T
    own = (0,)
    rest = tuple(range(1, n_tensor))
    gathered = pl.pallas_call(
        pack_kernel,
        out_shape=pltpu.VMEM((tok, full), BF),
        in_specs=[ANY] * 4,
        out_specs=VMEM,
        scratch_shapes=[
            pltpu.VMEM((2, tok), BF),
            pltpu.VMEM((2, tok), jnp.int32),
            pltpu.SemaphoreType.DMA((4,)),
        ],
        compiler_params=params(1),
        name="pack",
    )(*[pltpu.with_memory_space_constraint(x, pltpu.HBM) for x in (tokens, cotangent, gates.T, experts_t)])

    gate = w_gate[0]
    up, down = [pltpu.with_memory_space_constraint(w[0], pltpu.VMEM) for w in (w_up, w_down)]
    plan = [[(gate, True, own)], [(gate, True, rest)]]
    staged = []
    offsets = [0]
    mask = n_wide // 2
    while mask >= replicas:
        last = mask == replicas
        got = swap(gathered, mask, 0)
        jobs = sum(plan if last else plan[:1], [])
        plan = plan[1:]
        tokens_done = []
        if jobs:
            kept, token = stage(position, jobs, width, gathered)
            staged += kept
            tokens_done = [token]
        if not last:
            gathered = pl.pallas_call(
                join_kernel,
                out_shape=pltpu.VMEM((2 * gathered.shape[0], full), BF),
                in_specs=[VMEM] * 2 + [ANY] * len(tokens_done),
                out_specs=VMEM,
                compiler_params=params(2),
        name="join",
            )(gathered, got, *tokens_done)
        else:
            early = select(expert, gathered, len(offsets), position)
            every = offsets + [offset ^ mask for offset in offsets]
            order, *hits = pl.pallas_call(
                functools.partial(plan_kernel, replicas, every),
                out_shape=[pltpu.VMEM((2 * slots, 2 * slots), BF)] + [pltpu.VMEM((tok, 2 * slots), BF)] * 4,
                in_specs=[SMEM, VMEM, ANY],
                out_specs=[VMEM] * 5,
                compiler_params=params(4),
                name="plan",
            )(position, experts_t, early)
            late = select(expert, got, len(offsets), order)
        offsets = offsets + [offset ^ mask for offset in offsets]
        mask //= 2

    wg_own, wg_rest = staged
    pieces = [early, late]
    away = [[swap(piece, 0, m) for piece in pieces] for m in rest]
    near = pieces + [swap(piece, r, 0) for r in range(1, replicas) for piece in pieces]

    others = n_tensor - 1
    partial = pl.pallas_call(
        functools.partial(first_kernel, len(near)),
        out_shape=[shape(slots, hidden, F32)] * 2 + [shape(hidden // 2, 2 * slots, F32)],
        in_specs=[SMEM] + [VMEM] * (len(near) + 3),
        out_specs=[VMEM] * 3,
        compiler_params=params(5),
        cost_estimate=cost(24 * slots * width * hidden, 6 * width * hidden),
        name="first",
    )(position, *near, wg_own, up, down)

    parts = []
    for first_piece, second_piece in away:
        both = [first_piece, relay(second_piece, partial[0])]
        parts.append(both + [swap(piece, r, 0) for r in range(1, replicas) for piece in both])
    count = len(near)
    weighted, grad_gate, grad_up, inputs, upstream, score = pl.pallas_call(
        functools.partial(second_kernel, count, others),
        out_shape=[shape(slots, hidden)] * 3
        + [shape(slots, width * n_tensor)] * 2
        + [shape(1, slots, F32)],
        in_specs=[SMEM] + [VMEM] * (count * n_tensor + 6),
        out_specs=[VMEM] * 6,
        scratch_shapes=[pltpu.VMEM((2 * slots, hidden // 2), F32)],
        compiler_params=params(6),
        cost_estimate=cost(24 * slots * width * hidden, 6 * width * hidden),
        name="second",
    )(position, *near, *sum(parts, []), wg_rest, up, down, *partial)

    half = width // 2
    sent = pl.pallas_call(
        functools.partial(back_other_kernel, others),
        out_shape=[shape(half + 16, 2 * slots)] * others,
        in_specs=[SMEM] + [VMEM] * 5,
        out_specs=[VMEM] * others,
        compiler_params=params(5),
        cost_estimate=cost(16 * slots * width * hidden, 4 * width * hidden),
        name="back_other",
    )(position, grad_gate, grad_up, wg_rest, up, score)
    returned = [swap(value, 0, m) for m, value in zip(rest, sent)]
    kept = pl.pallas_call(
        back_own_kernel,
        out_shape=shape(half, 2 * slots, F32),
        in_specs=[SMEM] + [VMEM] * 5,
        out_specs=VMEM,
        compiler_params=params(5),
        cost_estimate=cost(16 * slots * width * hidden, 4 * width * hidden),
        name="back_own",
    )(position, grad_gate, grad_up, wg_own, up, score)
    (gate_proj_grad,) = outer([(inputs, grad_gate)], "gate_grad", 16)
    merged = pl.pallas_call(
        merge_kernel,
        out_shape=shape(2 * slots, half + LANES),
        in_specs=[ANY] + [VMEM] * (3 + others),
        out_specs=VMEM,
        compiler_params=params(4),
        name="merge",
    )(pltpu.with_memory_space_constraint(gate_proj_grad, pltpu.HBM), order, kept, score, *returned)
    landed = lax.all_to_all(merged, "wide", split_axis=0, concat_axis=0, tiled=True)
    up_proj_grad, down_proj_grad = outer([(inputs, grad_up), (weighted, upstream)], "other_grads")
    input_grad, routing_grad = pl.pallas_call(
        finish_kernel,
        out_shape=[shape(tok, width), shape(2, tok, F32)],
        in_specs=[VMEM] * 5,
        out_specs=[VMEM] * 2,
        compiler_params=params(3),
        name="finish",
    )(landed, *hits)
    return (
        input_grad,
        routing_grad.T,
        gate_proj_grad[None],
        up_proj_grad[None],
        down_proj_grad[None],
    )


def solution(mesh):
    return jax.shard_map(
        functools.partial(shards, mesh.shape["wide"], mesh.shape["tensor"]),
        mesh=mesh,
        in_specs=(
            P("wide", "tensor"),
            P("wide", "tensor"),
            P("wide", None),
            P("wide", None),
            P("wide", None, "tensor"),
            P("wide", None, "tensor"),
            P("wide", "tensor", None),
        ),
        out_specs=(
            P("wide", "tensor"),
            P("wide", None),
            P("wide", None, "tensor"),
            P("wide", None, "tensor"),
            P("wide", "tensor", None),
        ),
        check_vma=False,
    )
```

time: 76.3 us -> 64.2 us (0.84)
  Pallas kernels: 50.8 us -> 43.7 us
  waiting for transfers between devices: 6.94 us -> 3.89 us
  local copies, waits for them, and re-layouts: 2.81 us -> 0.02 us
  starting transfers between devices: 14.3 us -> 15.3 us
    pallas_call x10 -> x11, Pallas kernels: 32.3 us -> 24 us  [the longest x2 7.78 us: stage(): pl.pallas_call(functools.partial(stage_kernel, [job[1:] for job in jobs])...]
    ppermute x7 -> x10, waiting for transfers between devices: 6.94 us -> 3.89 us  [swap(): return lax.ppermute(value, axes, pairs)]
    unnamed x10, local copies, waits for them, and re-layouts: 2.81 us -> 0.02 us
    ppermute x7 -> x10, starting transfers between devices: 10.4 us -> 11.6 us  [swap(): return lax.ppermute(value, axes, pairs)]
  transfers between devices with their start and end apart: 8 -> 11, of which waited for: 2 -> 3; matrix products, arithmetic and copies ran while one was open for 0% -> 0% of each run, Pallas kernels for 50% -> 50%
where the time goes in v2:
time: 64.2 us; the launch traced here: 63.9 us
  Pallas kernels  43.7 us (68%)
  starting transfers between devices  15.3 us (24%)
  waiting for transfers between devices  3.89 us (6%)
  between operations  0.85 us (1%)
    pallas_call x2, Pallas kernels, outer(): pl.pallas_call(functools.partial(outer_kernel, tile, depth, len(pairs)),...  14.6 us
    ppermute x10, starting transfers between devices, swap(): return lax.ppermute(value, axes, pairs)  11.6 us
    pallas_call x2, Pallas kernels, stage(): pl.pallas_call(functools.partial(stage_kernel, [job[1:] for job in jobs])...  7.78 us
    pallas_call x1, Pallas kernels, shards(): pl.pallas_call(functools.partial(second_kernel, count, others), out_shape...  4.84 us
    pallas_call x1, Pallas kernels, shards(): pl.pallas_call(functools.partial(first_kernel, len(near)), out_shape=[sha...  4.39 us
    pallas_call x1, Pallas kernels, shards(): pl.pallas_call(functools.partial(back_other_kernel, others), out_shape=[s...  4.2 us
    pallas_call x1, Pallas kernels, shards(): pl.pallas_call(back_own_kernel, out_shape=shape(half, 2 * slots, F32), in...  3.95 us
    ppermute x10, waiting for transfers between devices, swap(): return lax.ppermute(value, axes, pairs)  3.89 us
  transfers between devices with their start and end apart: 11, of which 3 were waited for; matrix products, arithmetic and copies ran while one was open for 0% of the time, Pallas kernels for 50%

profile of v2, /device:TPU:0, one launch (start us, length us, event | category | flops | bytes accessed | tf_op | source)
XLA Modules:
  0.0 63.9 jit_solution(2507813035490986583)
XLA Ops:
  0.6 0.8 %pack.1.after_ref.own_ref = bf16[8,3200]{1,0:T(8,128)(2,1)S(1)} custom-call(bf16[8,1536]{1,0:T(8,128)(2,1)} %tokens_hbm.1, bf16[8,1536]{1,0:T(8,128)(2,1)} %cotangent_hbm.1, bf16[2,8]{1,0:T(2,128)(2,1)} %bitcast.28, s32[2,8]{1,0:T(2,128)} %bitcast.23), custom_call_target="tpu_custom_call" | custom-call | tf_op jit(solution)/shard_map/pack/pallas_call | solution.py:432
  1.5 4.1 %collective-permute-start = (bf16[8,3200]{1,0:T(8,128)(2,1)S(1)}, bf16[8,3200]{1,0:T(8,128)(2,1)S(1)}, u32[]{:S(2)}, u32[]{:S(2)}) collective-permute-start(bf16[8,3200]{1,0:T(8,128)(2,1)S(1)} %pack.1.after_ref.own_ref), channel_id=1, source_target_pairs={{0,8},{1,9},{2,10},{3,11},{4,12},{5,13},{6,14},{7,15},{8,0},{9,1},... | collective-permute-start | bytes 153608 | tf_op jit(solution)/shard_map/ppermute | solution.py:424
  5.6 0.1 pad_add_fusion.position_ref.refs_0_
  5.7 3.6 %stage.2 = (bf16[1536,2048]{1,0:T(8,128)(2,1)S(1)}, f32[8,128]{1,0:T(8,128)S(1)}) custom-call(s32[3]{0:T(128)S(1)} %pad_add_fusion.position_ref.refs_0_, bf16[8,3200]{1,0:T(8,128)(2,1)S(1)} %pack.1.after_ref.own_ref, bf16[3072,2048]{1,0:T(8,128)(2,1)} %bitcast.25), custom_call_target="tpu_custom_call" | custom-call | bytes 12582912 | tf_op jit(solution)/shard_map/stage/pallas_call | solution.py:126
  9.3 0.0 slice-start.2
  9.3 1.6 %collective-permute-start.1 = (bf16[16,3200]{1,0:T(8,128)(2,1)S(1)}, bf16[16,3200]{1,0:T(8,128)(2,1)S(1)}, u32[]{:S(2)}, u32[]{:S(2)}) collective-permute-start(bf16[16,3200]{1,0:T(8,128)(2,1)S(1)} %join.2.after_ref.own_ref), channel_id=1, source_target_pairs={{0,4},{1,5},{2,6},{3,7},{4,0},{5,1},{6,2},{7,3},{8,12},{9,13},{10,... | collective-permute-start | bytes 307208 | tf_op jit(solution)/shard_map/ppermute | solution.py:424
  11.0 4.2 %stage.3 = (bf16[1536,2048]{1,0:T(8,128)(2,1)S(1)}, f32[8,128]{1,0:T(8,128)S(1)}) custom-call(s32[3]{0:T(128)S(1)} %pad_add_fusion.position_ref.refs_0_, bf16[16,3200]{1,0:T(8,128)(2,1)S(1)} %join.2.after_ref.own_ref, bf16[3072,2048]{1,0:T(8,128)(2,1)} %bitcast.26), custom_call_target="tpu_custom_call" | custom-call | bytes 12582912 | tf_op jit(solution)/shard_map/stage/pallas_call | solution.py:126
  15.2 1.6 %collective-permute-start.2 = (bf16[32,3200]{1,0:T(8,128)(2,1)S(1)}, bf16[32,3200]{1,0:T(8,128)(2,1)S(1)}, u32[]{:S(2)}, u32[]{:S(2)}) collective-permute-start(bf16[32,3200]{1,0:T(8,128)(2,1)S(1)} %join.3.source_ref), channel_id=1, source_target_pairs={{0,2},{1,3},{2,0},{3,1},{4,6},{5,7},{6,4},{7,5},{8,10},{9,11},{10,... | collective-permute-start | bytes 614408 | tf_op jit(solution)/shard_map/ppermute | solution.py:424
  16.8 0.3 select.6.after_ref.refs_0_
  17.1 0.6 plan.1
  17.7 1.6 %collective-permute-start.5 = (bf16[16,3200]{1,0:T(8,128)(2,1)S(1)}, bf16[16,3200]{1,0:T(8,128)(2,1)S(1)}, u32[]{:S(2)}, u32[]{:S(2)}) collective-permute-start(bf16[16,3200]{1,0:T(8,128)(2,1)S(1)} %select.6.after_ref.refs_0_), channel_id=1, source_target_pairs={{0,16},{1,17},{2,18},{3,19},{4,20},{5,21},{6,22},{7,23},{8,24},{9,... | collective-permute-start | bytes 307208 | tf_op jit(solution)/shard_map/ppermute | solution.py:424
  19.2 0.0 collective-permute-start.3
  19.2 2.2 %collective-permute-done.2.source_ref = bf16[32,3200]{1,0:T(8,128)(2,1)S(1)} collective-permute-done((bf16[32,3200]{1,0:T(8,128)(2,1)S(1)}, bf16[32,3200]{1,0:T(8,128)(2,1)S(1)}, u32[]{:S(2)}, u32[]{:S(2)}) %collective-permute-start.2) | collective-permute-done | bytes 204832 | tf_op jit(solution)/shard_map/ppermute | solution.py:424
  21.5 0.3 select.7.refs_1_
  21.8 0.1 collective-permute-start.4
  21.9 0.6 collective-permute-done.5.refs_4_
  22.4 1.5 %collective-permute-start.6 = (bf16[16,3200]{1,0:T(8,128)(2,1)S(1)}, bf16[16,3200]{1,0:T(8,128)(2,1)S(1)}, u32[]{:S(2)}, u32[]{:S(2)}) collective-permute-start(bf16[16,3200]{1,0:T(8,128)(2,1)S(1)} %select.7.refs_1_), channel_id=1, source_target_pairs={{0,16},{1,17},{2,18},{3,19},{4,20},{5,21},{6,22},{7,23},{8,24},{9,... | collective-permute-start | bytes 307208 | tf_op jit(solution)/shard_map/ppermute | solution.py:424
  23.9 0.0 collective-permute-done.3.refs_2_
  23.9 0.0 collective-permute-done.4.refs_3_
  24.0 4.4 %first.1 = (f32[64,2048]{1,0:T(8,128)S(1)}, f32[64,2048]{1,0:T(8,128)S(1)}, f32[1024,128]{1,0:T(8,128)S(1)}) custom-call(s32[3]{0:T(128)S(1)} %pad_add_fusion.position_ref.refs_0_, bf16[16,3200]{1,0:T(8,128)(2,1)S(1)} %select.6.after_ref.refs_0_, bf16[16,3200]{1,0:T(8,128)(2,1)S(1)} %select.7.refs_1_, bf16[16,3200]{1,0:T(8,128)(2,1)S(1)} %collective-permute-done.3.refs_2_, ...), custom_call_target="tpu_custom_call" | custom-call | flops 4831838208 | bytes 18874368 | tf_op jit(solution)/shard_map/first/pallas_call | solution.py:492
  28.4 0.3 collective-permute-start.8
  28.7 0.0 collective-permute-done.7.refs_6_
  28.7 1.1 %collective-permute-done.8.refs_7_ = bf16[16,3200]{1,0:T(8,128)(2,1)S(1)} collective-permute-done((bf16[16,3200]{1,0:T(8,128)(2,1)S(1)}, bf16[16,3200]{1,0:T(8,128)(2,1)S(1)}, u32[]{:S(2)}, u32[]{:S(2)}) %collective-permute-start.8) | collective-permute-done | bytes 102432 | tf_op jit(solution)/shard_map/ppermute | solution.py:424
  29.8 4.8 %second.1 = (bf16[64,2048]{1,0:T(8,128)(2,1)S(1)}, bf16[64,2048]{1,0:T(8,128)(2,1)S(1)}, bf16[64,2048]{1,0:T(8,128)(2,1)S(1)}, bf16[64,3072]{1,0:T(8,128)(2,1)S(...) custom-call(s32[3]{0:T(128)S(1)} %pad_add_fusion.position_ref.refs_0_, ...), custom_call_target="tpu_custom_call" | custom-call | flops 4831838208 | bytes 18874368 | tf_op jit(solution)/shard_map/second/pallas_call | solution.py:507
  34.6 4.2 %back_other.1 = bf16[784,128]{1,0:T(8,128)(2,1)S(1)} custom-call(s32[3]{0:T(128)S(1)} %pad_add_fusion.position_ref.refs_0_, bf16[64,2048]{1,0:T(8,128)(2,1)S(1)} %get-tuple-element.36.refs_1_.refs_0_, bf16[64,2048]{1,0:T(8,128)(2,1)S(1)} %get-tuple-element.37.refs_1_.refs_2_, bf16[1536,2048]{1,0:T(8,128)(2,1)S(1)} %get-tuple-element.32.refs_8_.refs_2_, ...), custom_call_target="tpu_custom_call" | custom-call | flops 3221225472 | bytes 12582912 | tf_op jit(solution)/shard_map/back_other/pallas_call | solution.py:521
  38.8 0.8 %collective-permute-start.9 = (bf16[784,128]{1,0:T(8,128)(2,1)S(1)}, bf16[784,128]{1,0:T(8,128)(2,1)S(1)}, u32[]{:S(2)}, u32[]{:S(2)}) collective-permute-start(bf16[784,128]{1,0:T(8,128)(2,1)S(1)} %back_other.1), channel_id=1, source_target_pairs={{0,16},{1,17},{2,18},{3,19},{4,20},{5,21},{6,22},{7,23},{8,24},{9,... | collective-permute-start | bytes 602120 | tf_op jit(solution)/shard_map/ppermute | solution.py:424
  39.6 5.4 %gate_grad.1.after_ref = bf16[3072,2048]{1,0:T(8,128)(2,1)} custom-call(bf16[64,3072]{1,0:T(8,128)(2,1)S(1)} %get-tuple-element.35.refs_0_, bf16[64,2048]{1,0:T(8,128)(2,1)S(1)} %get-tuple-element.36.refs_1_.refs_0_), custom_call_target="tpu_custom_call" | custom-call | flops 201326592 | bytes 786432 | tf_op jit(solution)/shard_map/gate_grad/pallas_call | solution.py:391
  45.0 4.0 %back_own.1.own_ref = f32[768,128]{1,0:T(8,128)S(1)} custom-call(s32[3]{0:T(128)S(1)} %pad_add_fusion.position_ref.refs_0_, bf16[64,2048]{1,0:T(8,128)(2,1)S(1)} %get-tuple-element.36.refs_1_.refs_0_, bf16[64,2048]{1,0:T(8,128)(2,1)S(1)} %get-tuple-element.37.refs_1_.refs_2_, bf16[1536,2048]{1,0:T(8,128)(2,1)S(1)} %get-tuple-element.30.refs_4_.refs_2_, ...), custom_call_target="tpu_custom_call" | custom-call | flops 3221225472 | bytes 12582912 | tf_op jit(solution)/shard_map/back_own/pallas_call | solution.py:531
  49.0 1.0 %merge.1 = bf16[128,896]{1,0:T(8,128)(2,1)} custom-call(bf16[3072,2048]{1,0:T(8,128)(2,1)} %gate_grad.1.after_ref, bf16[128,128]{1,0:T(8,128)(2,1)S(1)} %get-tuple-element.29.refs_0_.order_ref, f32[768,128]{1,0:T(8,128)S(1)} %back_own.1.own_ref, f32[1,64]{1,0:T(1,128)S(1)} %get-tuple-element.38.refs_4_.routing_ref, ...), custom_call_target="tpu_custom_call" | custom-call | tf_op jit(solution)/shard_map/merge/pallas_call | solution.py:541
  50.0 3.7 %all-to-all-start = ((bf16[16,8,896]{2,1,0:T(8,128)(2,1)}), bf16[16,8,896]{2,1,0:T(8,128)(2,1)S(1)}, u32[]{:S(2)}, u32[]{:S(2)}) async-start(bf16[16,8,896]{2,1,0:T(8,128)(2,1)} %bitcast.8), calls=%async_computation | async-start | bytes 458752 | tf_op jit(solution)/shard_map/all_to_all | solution.py:549
  53.7 9.3 %other_grads.1 = (bf16[3072,2048]{1,0:T(8,128)(2,1)}, bf16[2048,3072]{1,0:T(8,128)(2,1)}) custom-call(bf16[64,3072]{1,0:T(8,128)(2,1)S(1)} %get-tuple-element.35.refs_0_, bf16[64,2048]{1,0:T(8,128)(2,1)S(1)} %get-tuple-element.45.refs_1_, bf16[64,2048]{1,0:T(8,128)(2,1)S(1)} %get-tuple-element.37.refs_1_.refs_2_, bf16[64,3072]{1,0:T(8,128)(2,1)S(1)} %get-tuple-element.46.refs_3_), custom_call_target="tpu_custom_call" | custom-call | flops 6442450944 | bytes 25165824 | tf_op jit(solution)/shard_map/other_grads/pallas_call | solution.py:391
  63.0 0.8 %finish.1 = (bf16[8,1536]{1,0:T(8,128)(2,1)}, f32[2,8]{1,0:T(2,128)}) custom-call(bf16[128,896]{1,0:T(8,128)(2,1)S(1)} %bitcast.22, bf16[8,128]{1,0:T(8,128)(2,1)S(1)} %get-tuple-element.39.low_ref, bf16[8,128]{1,0:T(8,128)(2,1)S(1)} %get-tuple-element.40.high_ref, bf16[8,128]{1,0:T(8,128)(2,1)S(1)} %get-tuple-element.41.first_ref, ...), custom_call_target="tpu_custom_call" | custom-call | tf_op jit(solution)/shard_map/finish/pallas_call | solution.py:551
  (19 shorter events, 0.1 us)
Async XLA Ops:
  1.5 7.8 %collective-permute-start = (bf16[8,3200]{1,0:T(8,128)(2,1)S(1)}, bf16[8,3200]{1,0:T(8,128)(2,1)S(1)}, u32[]{:S(2)}, u32[]{:S(2)}) collective-permute-start(bf16[8,3200]{1,0:T(8,128)(2,1)S(1)} %pack.1.after_ref.own_ref), channel_id=1, source_target_pairs={{0,8},{1,9},{2,10},{3,11},{4,12},{5,13},{6,14},{7,15},{8,0},{9,1},... | collective-permute-start | bytes 153608 | tf_op jit(solution)/shard_map/ppermute | solution.py:424
  5.6 11.4 %copy-start.1 = (s32[8,2]{0,1:T(2,128)S(1)}, s32[8,2]{0,1:T(2,128)}, u32[]{:S(2)}) copy-start(s32[8,2]{0,1:T(2,128)} %param.10) | copy-start | bytes 196
  5.6 18.3 %slice-start = ((s8[12582912]{0:T(1024)(128)(4,1)}), s8[4194304]{0:T(1024)(128)(4,1)S(1)}, s32[]{:S(2)}) async-start(s8[12582912]{0:T(1024)(128)(4,1)} %bitcast.14), calls=%async_computation.1 | async-start | bytes 8388608
  5.6 18.3 %slice-start.1 = ((s8[12582912]{0:T(1024)(128)(4,1)}), s8[4194304]{0:T(1024)(128)(4,1)S(1)}, s32[]{:S(2)}) async-start(s8[12582912]{0:T(1024)(128)(4,1)} %bitcast.14), calls=%async_computation.2 | async-start | bytes 8388608
  5.6 18.3 %copy-start = (bf16[1,2048,3072]{2,1,0:T(8,128)(2,1)S(1)}, bf16[1,2048,3072]{2,1,0:T(8,128)(2,1)}, u32[]{:S(2)}) copy-start(bf16[1,2048,3072]{2,1,0:T(8,128)(2,1)} %param.13) | copy-start | bytes 37748740
  9.3 14.6 %slice-start.2 = ((s8[12582912]{0:T(1024)(128)(4,1)}), s8[4194304]{0:T(1024)(128)(4,1)S(1)}, s32[]{:S(2)}) async-start(s8[12582912]{0:T(1024)(128)(4,1)} %bitcast.14), calls=%async_computation.3 | async-start | bytes 8388608
  9.3 5.8 %collective-permute-start.1 = (bf16[16,3200]{1,0:T(8,128)(2,1)S(1)}, bf16[16,3200]{1,0:T(8,128)(2,1)S(1)}, u32[]{:S(2)}, u32[]{:S(2)}) collective-permute-start(bf16[16,3200]{1,0:T(8,128)(2,1)S(1)} %join.2.after_ref.own_ref), channel_id=1, source_target_pairs={{0,4},{1,5},{2,6},{3,7},{4,0},{5,1},{6,2},{7,3},{8,12},{9,13},{10,... | collective-permute-start | bytes 307208 | tf_op jit(solution)/shard_map/ppermute | solution.py:424
  15.2 6.3 %collective-permute-start.2 = (bf16[32,3200]{1,0:T(8,128)(2,1)S(1)}, bf16[32,3200]{1,0:T(8,128)(2,1)S(1)}, u32[]{:S(2)}, u32[]{:S(2)}) collective-permute-start(bf16[32,3200]{1,0:T(8,128)(2,1)S(1)} %join.3.source_ref), channel_id=1, source_target_pairs={{0,2},{1,3},{2,0},{3,1},{4,6},{5,7},{6,4},{7,5},{8,10},{9,11},{10,... | collective-permute-start | bytes 614408 | tf_op jit(solution)/shard_map/ppermute | solution.py:424
  17.7 4.7 %collective-permute-start.5 = (bf16[16,3200]{1,0:T(8,128)(2,1)S(1)}, bf16[16,3200]{1,0:T(8,128)(2,1)S(1)}, u32[]{:S(2)}, u32[]{:S(2)}) collective-permute-start(bf16[16,3200]{1,0:T(8,128)(2,1)S(1)} %select.6.after_ref.refs_0_), channel_id=1, source_target_pairs={{0,16},{1,17},{2,18},{3,19},{4,20},{5,21},{6,22},{7,23},{8,24},{9,... | collective-permute-start | bytes 307208 | tf_op jit(solution)/shard_map/ppermute | solution.py:424
  19.2 4.7 %collective-permute-start.3 = (bf16[16,3200]{1,0:T(8,128)(2,1)S(1)}, bf16[16,3200]{1,0:T(8,128)(2,1)S(1)}, u32[]{:S(2)}, u32[]{:S(2)}) collective-permute-start(bf16[16,3200]{1,0:T(8,128)(2,1)S(1)} %select.6.after_ref.refs_0_), channel_id=1, source_target_pairs={{0,1},{1,0},{2,3},{3,2},{4,5},{5,4},{6,7},{7,6},{8,9},{9,8},{10,11... | collective-permute-start | bytes 307208 | tf_op jit(solution)/shard_map/ppermute | solution.py:424
  21.8 2.1 %collective-permute-start.4 = (bf16[16,3200]{1,0:T(8,128)(2,1)S(1)}, bf16[16,3200]{1,0:T(8,128)(2,1)S(1)}, u32[]{:S(2)}, u32[]{:S(2)}) collective-permute-start(bf16[16,3200]{1,0:T(8,128)(2,1)S(1)} %select.7.refs_1_), channel_id=1, source_target_pairs={{0,1},{1,0},{2,3},{3,2},{4,5},{5,4},{6,7},{7,6},{8,9},{9,8},{10,11... | collective-permute-start | bytes 307208 | tf_op jit(solution)/shard_map/ppermute | solution.py:424
  22.4 6.3 %collective-permute-start.7 = (bf16[16,3200]{1,0:T(8,128)(2,1)S(1)}, bf16[16,3200]{1,0:T(8,128)(2,1)S(1)}, u32[]{:S(2)}, u32[]{:S(2)}) collective-permute-start(bf16[16,3200]{1,0:T(8,128)(2,1)S(1)} %collective-permute-done.5.refs_4_), channel_id=1, source_target_pairs={{0,1},{1,0},{2,3},{3,2},{4,5},{5,4},{6,7},{7,6},{8,9},{9,8},{10,11... | collective-permute-start | bytes 307208 | tf_op jit(solution)/shard_map/ppermute | solution.py:424
  22.4 5.9 %collective-permute-start.6 = (bf16[16,3200]{1,0:T(8,128)(2,1)S(1)}, bf16[16,3200]{1,0:T(8,128)(2,1)S(1)}, u32[]{:S(2)}, u32[]{:S(2)}) collective-permute-start(bf16[16,3200]{1,0:T(8,128)(2,1)S(1)} %select.7.refs_1_), channel_id=1, source_target_pairs={{0,16},{1,17},{2,18},{3,19},{4,20},{5,21},{6,22},{7,23},{8,24},{9,... | collective-permute-start | bytes 307208 | tf_op jit(solution)/shard_map/ppermute | solution.py:424
  28.4 1.4 %collective-permute-start.8 = (bf16[16,3200]{1,0:T(8,128)(2,1)S(1)}, bf16[16,3200]{1,0:T(8,128)(2,1)S(1)}, u32[]{:S(2)}, u32[]{:S(2)}) collective-permute-start(bf16[16,3200]{1,0:T(8,128)(2,1)S(1)} %relay.1.refs_5_), channel_id=1, source_target_pairs={{0,1},{1,0},{2,3},{3,2},{4,5},{5,4},{6,7},{7,6},{8,9},{9,8},{10,11... | collective-permute-start | bytes 307208 | tf_op jit(solution)/shard_map/ppermute | solution.py:424
  38.8 10.2 %collective-permute-start.9 = (bf16[784,128]{1,0:T(8,128)(2,1)S(1)}, bf16[784,128]{1,0:T(8,128)(2,1)S(1)}, u32[]{:S(2)}, u32[]{:S(2)}) collective-permute-start(bf16[784,128]{1,0:T(8,128)(2,1)S(1)} %back_other.1), channel_id=1, source_target_pairs={{0,16},{1,17},{2,18},{3,19},{4,20},{5,21},{6,22},{7,23},{8,24},{9,... | collective-permute-start | bytes 602120 | tf_op jit(solution)/shard_map/ppermute | solution.py:424
  50.0 13.0 %all-to-all-start = ((bf16[16,8,896]{2,1,0:T(8,128)(2,1)}), bf16[16,8,896]{2,1,0:T(8,128)(2,1)S(1)}, u32[]{:S(2)}, u32[]{:S(2)}) async-start(bf16[16,8,896]{2,1,0:T(8,128)(2,1)} %bitcast.8), calls=%async_computation | async-start | bytes 458752 | tf_op jit(solution)/shard_map/all_to_all | solution.py:549

commit v3 on v2

--- a/solution.py
+++ b/solution.py
@@ -143,19 +143,15 @@
     out_ref[rows:, :] = got_ref[...]
 
 
-def relay_kernel(value_ref, *refs):
-    refs[-1][...] = value_ref[...]
-
-
-def relay(value, after):
+def join(first, second, after):
     return pl.pallas_call(
-        relay_kernel,
-        out_shape=pltpu.VMEM(value.shape, value.dtype),
-        in_specs=[VMEM, ANY],
+        join_kernel,
+        out_shape=pltpu.VMEM((first.shape[0] + second.shape[0], first.shape[1]), BF),
+        in_specs=[VMEM, VMEM, ANY],
         out_specs=VMEM,
         compiler_params=params(2),
-        name="relay",
-    )(value, after)
+        name="join",
+    )(first, second, after)
 
 
 def select_kernel(expert_ref, source_ref, *refs):
@@ -275,22 +271,13 @@
     width = w_gate.shape[0]
     half = width // 2
 
-    def products(rows):
-        part = folded(w_gate, *low_high(grad_gate[...])) + folded(w_up.at[rows], *low_high(grad_up[...]))
-        out_ref[:half, :] = part.astype(out_ref.dtype)
-
-    places = w_up.shape[0] // width
-    if places == 2:
-        for place in range(places):
-            pl.when(position ^ mask == place)(functools.partial(products, pl.ds(place * width, width)))
-    else:
-        products(pl.ds(pl.multiple_of((position ^ mask) * width, width), width))
+    gate_rows, up_rows = low_high(grad_gate[...]), low_high(grad_up[...])
+
+    rows = pl.ds(pl.multiple_of((position ^ mask) * width, width), width)
+    part = folded(w_gate, *gate_rows) + folded(w_up.at[rows], *up_rows)
+    out_ref[:half, :] = part.astype(out_ref.dtype)
     if out_ref.shape[0] > half:
         out_ref[half:, :] = halves(routing_ref[...], out_ref.shape[0] - half)
-
-
-def back_own_kernel(position_ref, *refs):
-    back(position_ref[0], 0, *refs)
 
 
 def back_other_kernel(others, position_ref, *refs):
@@ -302,7 +289,7 @@
         back(position_ref[0], m + 1, grad_gate, grad_up, w_gate.at[rows], w_up, routing_ref, out_ref)
 
 
-def merge_kernel(after_ref, order_ref, own_ref, routing_ref, *refs):
+def merge_kernel(order_ref, own_ref, routing_ref, *refs):
     parts, out_ref = refs[:-1], refs[-1]
     half, lanes = own_ref.shape
     slots = lanes // 2
@@ -358,7 +345,18 @@
 
 def outer_kernel(tile, depth, count, *refs):
     lefts, rights, outs = refs[:count], refs[count : 2 * count], refs[2 * count : 3 * count]
-    buffer, turned, sems = refs[3 * count :]
+    for copy in outer_copies(tile, depth, lefts, rights, outs, *refs[3 * count :]):
+        copy.wait()
+
+
+def outer_back_kernel(tile, depth, position_ref, left, right, grad_up, w_gate, w_up, score_ref, out, kept, *scratch):
+    pending = outer_copies(tile, depth, [left], [right], [out], *scratch)
+    back(position_ref[0], 0, right, grad_up, w_gate, w_up, score_ref, kept)
+    for copy in pending:
+        copy.wait()
+
+
+def outer_copies(tile, depth, lefts, rights, outs, buffer, turned, sems):
     steps = []
     for left, right, out in zip(lefts, rights, outs):
         rows, columns = out.shape
@@ -375,31 +373,36 @@
         place[...] = dot(turned[start : start + tile, :], right[...], 1, 0).astype(BF)
         copies.append(pltpu.make_async_copy(place, out.at[pl.ds(start, tile)], sems.at[slot]))
         copies[i].start()
-    for copy in copies[max(0, len(copies) - depth) :]:
-        copy.wait()
-
-
-def outer(pairs, name, weight=1):
-    shapes = [(left.shape[1], right.shape[1]) for left, right in pairs]
+    return copies[max(0, len(copies) - depth) :]
+
+
+def outer_plan(shapes, slots):
     tile = min([512] + [rows for rows, _ in shapes])
     tile = next(size for size in (tile, 384, 256, 128) if all(rows % size == 0 for rows, _ in shapes))
-    slots = pairs[0][0].shape[0]
     depth = 4
     widest = max(columns for _, columns in shapes)
     tallest = max(rows for rows, _ in shapes)
+    scratch = [
+        pltpu.VMEM((depth, tile, widest), BF),
+        pltpu.VMEM((tallest, slots), BF),
+        pltpu.SemaphoreType.DMA((depth,)),
+    ]
+    return tile, depth, scratch
+
+
+def outer(pairs, name):
+    shapes = [(left.shape[1], right.shape[1]) for left, right in pairs]
+    slots = pairs[0][0].shape[0]
+    tile, depth, scratch = outer_plan(shapes, slots)
     size = sum(rows * columns for rows, columns in shapes)
     return pl.pallas_call(
         functools.partial(outer_kernel, tile, depth, len(pairs)),
         out_shape=[jax.ShapeDtypeStruct(shape, BF) for shape in shapes],
         in_specs=[VMEM] * (2 * len(pairs)),
         out_specs=[ANY] * len(pairs),
-        scratch_shapes=[
-            pltpu.VMEM((depth, tile, widest), BF),
-            pltpu.VMEM((tallest, slots), BF),
-            pltpu.SemaphoreType.DMA((depth,)),
-        ],
+        scratch_shapes=scratch,
         compiler_params=params(20),
-        cost_estimate=cost(8 * slots * size // weight, 2 * size // weight),
+        cost_estimate=cost(8 * slots * size, 2 * size),
         name=name,
     )(*[left for left, _ in pairs], *[right for _, right in pairs])
 
@@ -454,20 +457,11 @@
         got = swap(gathered, mask, 0)
         jobs = sum(plan if last else plan[:1], [])
         plan = plan[1:]
-        tokens_done = []
         if jobs:
             kept, token = stage(position, jobs, width, gathered)
             staged += kept
-            tokens_done = [token]
         if not last:
-            gathered = pl.pallas_call(
-                join_kernel,
-                out_shape=pltpu.VMEM((2 * gathered.shape[0], full), BF),
-                in_specs=[VMEM] * 2 + [ANY] * len(tokens_done),
-                out_specs=VMEM,
-                compiler_params=params(2),
-        name="join",
-            )(gathered, got, *tokens_done)
+            gathered = join(gathered, got, token if jobs else got)
         else:
             early = select(expert, gathered, len(offsets), position)
             every = offsets + [offset ^ mask for offset in offsets]
@@ -484,9 +478,9 @@
         mask //= 2
 
     wg_own, wg_rest = staged
-    pieces = [early, late]
-    away = [[swap(piece, 0, m) for piece in pieces] for m in rest]
-    near = pieces + [swap(piece, r, 0) for r in range(1, replicas) for piece in pieces]
+    away = [[swap(early, 0, m), swap(late, 0, m)] for m in rest]
+    chosen = join(early, late, away[0][0])
+    near = [chosen] + [swap(chosen, r, 0) for r in range(1, replicas)]
 
     others = n_tensor - 1
     partial = pl.pallas_call(
@@ -495,14 +489,14 @@
         in_specs=[SMEM] + [VMEM] * (len(near) + 3),
         out_specs=[VMEM] * 3,
         compiler_params=params(5),
-        cost_estimate=cost(24 * slots * width * hidden, 6 * width * hidden),
+        cost_estimate=cost(2 * slots * width * hidden, width * hidden // 2),
         name="first",
     )(position, *near, wg_own, up, down)
 
     parts = []
-    for first_piece, second_piece in away:
-        both = [first_piece, relay(second_piece, partial[0])]
-        parts.append(both + [swap(piece, r, 0) for r in range(1, replicas) for piece in both])
+    for early_part, late_part in away:
+        part = join(early_part, late_part, partial[0])
+        parts.append([part] + [swap(part, r, 0) for r in range(1, replicas)])
     count = len(near)
     weighted, grad_gate, grad_up, inputs, upstream, score = pl.pallas_call(
         functools.partial(second_kernel, count, others),
@@ -528,24 +522,26 @@
         name="back_other",
     )(position, grad_gate, grad_up, wg_rest, up, score)
     returned = [swap(value, 0, m) for m, value in zip(rest, sent)]
-    kept = pl.pallas_call(
-        back_own_kernel,
-        out_shape=shape(half, 2 * slots, F32),
-        in_specs=[SMEM] + [VMEM] * 5,
-        out_specs=VMEM,
-        compiler_params=params(5),
-        cost_estimate=cost(16 * slots * width * hidden, 4 * width * hidden),
-        name="back_own",
-    )(position, grad_gate, grad_up, wg_own, up, score)
-    (gate_proj_grad,) = outer([(inputs, grad_gate)], "gate_grad", 16)
+    grad_shape = (inputs.shape[1], hidden)
+    tile, depth, scratch = outer_plan([grad_shape], slots)
+    gate_proj_grad, kept = pl.pallas_call(
+        functools.partial(outer_back_kernel, tile, depth),
+        out_shape=[jax.ShapeDtypeStruct(grad_shape, BF), shape(half, 2 * slots, F32)],
+        in_specs=[SMEM] + [VMEM] * 6,
+        out_specs=[ANY, VMEM],
+        scratch_shapes=scratch,
+        compiler_params=params(16),
+        cost_estimate=cost(8 * slots * grad_shape[0] * hidden, 2 * grad_shape[0] * hidden),
+        name="gate_grad",
+    )(position, inputs, grad_gate, grad_up, wg_own, up, score)
     merged = pl.pallas_call(
         merge_kernel,
         out_shape=shape(2 * slots, half + LANES),
-        in_specs=[ANY] + [VMEM] * (3 + others),
+        in_specs=[VMEM] * (3 + others),
         out_specs=VMEM,
         compiler_params=params(4),
         name="merge",
-    )(pltpu.with_memory_space_constraint(gate_proj_grad, pltpu.HBM), order, kept, score, *returned)
+    )(order, kept, score, *returned)
     landed = lax.all_to_all(merged, "wide", split_axis=0, concat_axis=0, tiled=True)
     up_proj_grad, down_proj_grad = outer([(inputs, grad_up), (weighted, upstream)], "other_grads")
     input_grad, routing_grad = pl.pallas_call(

time: 64.2 us -> 62.7 us (0.977)
  Pallas kernels: 43.7 us -> 41.9 us
    pallas_call x2 -> x1, Pallas kernels: 14.6 us -> 9.29 us  [outer(): pl.pallas_call(functools.partial(outer_kernel, tile, depth, len(pairs)),...]
    pallas_call x4 -> x5, Pallas kernels: 3.99 us -> 7.84 us  [the longest x1 7.78 us: shards(): pl.pallas_call(functools.partial(outer_back_kernel, tile, depth), out_sha...]
    ppermute x10 -> x8, starting transfers between devices: 11.6 us -> 12.2 us  [swap(): return lax.ppermute(value, axes, pairs)]
    ppermute x10 -> x8, waiting for transfers between devices: 3.89 us -> 3.56 us  [swap(): return lax.ppermute(value, axes, pairs)]
  transfers between devices with their start and end apart: 11 -> 9, of which waited for: 3 -> 3; matrix products, arithmetic and copies ran while one was open for 0% -> 0% of each run, Pallas kernels for 50% -> 49%
where the time goes in v3:
time: 62.7 us; the launch traced here: 62.4 us
  Pallas kernels  41.9 us (67%)
  starting transfers between devices  15.8 us (25%)
  waiting for transfers between devices  3.78 us (6%)
  between operations  0.84 us (1%)
    ppermute x8, starting transfers between devices, swap(): return lax.ppermute(value, axes, pairs)  12.2 us
    pallas_call x1, Pallas kernels, outer(): pl.pallas_call(functools.partial(outer_kernel, tile, depth, len(pairs)),...  9.29 us
    pallas_call x1, Pallas kernels, shards(): pl.pallas_call(functools.partial(outer_back_kernel, tile, depth), out_sha...  7.78 us
    pallas_call x2, Pallas kernels, stage(): pl.pallas_call(functools.partial(stage_kernel, [job[1:] for job in jobs])...  7.78 us
    pallas_call x1, Pallas kernels, shards(): pl.pallas_call(functools.partial(second_kernel, count, others), out_shape...  4.86 us
    pallas_call x1, Pallas kernels, shards(): pl.pallas_call(functools.partial(first_kernel, len(near)), out_shape=[sha...  4.39 us
    pallas_call x1, Pallas kernels, shards(): pl.pallas_call(functools.partial(back_other_kernel, others), out_shape=[s...  3.93 us
    all_to_all x1, starting transfers between devices, shards(): lax.all_to_all(merged, 'wide', split_axis=0, concat_axis=0, tiled=True)  3.56 us
  transfers between devices with their start and end apart: 9, of which 3 were waited for; matrix products, arithmetic and copies ran while one was open for 0% of the time, Pallas kernels for 49%

profile of v3, /device:TPU:0, one launch (start us, length us, event | category | flops | bytes accessed | tf_op | source)
XLA Modules:
  0.0 62.4 jit_solution(5005365677156006779)
XLA Ops:
  0.6 0.8 %pack.1.after_ref.own_ref = bf16[8,3200]{1,0:T(8,128)(2,1)S(1)} custom-call(bf16[8,1536]{1,0:T(8,128)(2,1)} %tokens_hbm.1, bf16[8,1536]{1,0:T(8,128)(2,1)} %cotangent_hbm.1, bf16[2,8]{1,0:T(2,128)(2,1)} %bitcast.27, s32[2,8]{1,0:T(2,128)} %bitcast.23), custom_call_target="tpu_custom_call" | custom-call | tf_op jit(solution)/shard_map/pack/pallas_call | solution.py:435
  1.5 4.1 %collective-permute-start = (bf16[8,3200]{1,0:T(8,128)(2,1)S(1)}, bf16[8,3200]{1,0:T(8,128)(2,1)S(1)}, u32[]{:S(2)}, u32[]{:S(2)}) collective-permute-start(bf16[8,3200]{1,0:T(8,128)(2,1)S(1)} %pack.1.after_ref.own_ref), channel_id=1, source_target_pairs={{0,8},{1,9},{2,10},{3,11},{4,12},{5,13},{6,14},{7,15},{8,0},{9,1},... | collective-permute-start | bytes 153608 | tf_op jit(solution)/shard_map/ppermute | solution.py:427
  5.6 0.1 pad_add_fusion.position_ref.refs_0_
  5.7 3.6 %stage.2 = (bf16[1536,2048]{1,0:T(8,128)(2,1)S(1)}, f32[8,128]{1,0:T(8,128)S(1)}) custom-call(s32[3]{0:T(128)S(1)} %pad_add_fusion.position_ref.refs_0_, bf16[8,3200]{1,0:T(8,128)(2,1)S(1)} %pack.1.after_ref.own_ref, bf16[3072,2048]{1,0:T(8,128)(2,1)} %bitcast.25), custom_call_target="tpu_custom_call" | custom-call | bytes 12582912 | tf_op jit(solution)/shard_map/stage/pallas_call | solution.py:126
  9.3 0.0 collective-permute-done.got_ref
  9.3 0.0 slice-start.2
  9.3 1.6 %collective-permute-start.1 = (bf16[16,3200]{1,0:T(8,128)(2,1)S(1)}, bf16[16,3200]{1,0:T(8,128)(2,1)S(1)}, u32[]{:S(2)}, u32[]{:S(2)}) collective-permute-start(bf16[16,3200]{1,0:T(8,128)(2,1)S(1)} %join.4.after_ref.own_ref), channel_id=1, source_target_pairs={{0,4},{1,5},{2,6},{3,7},{4,0},{5,1},{6,2},{7,3},{8,12},{9,13},{10,... | collective-permute-start | bytes 307208 | tf_op jit(solution)/shard_map/ppermute | solution.py:427
  11.0 4.2 %stage.3 = (bf16[1536,2048]{1,0:T(8,128)(2,1)S(1)}, f32[8,128]{1,0:T(8,128)S(1)}) custom-call(s32[3]{0:T(128)S(1)} %pad_add_fusion.position_ref.refs_0_, bf16[16,3200]{1,0:T(8,128)(2,1)S(1)} %join.4.after_ref.own_ref, bf16[3072,2048]{1,0:T(8,128)(2,1)} %bitcast.26), custom_call_target="tpu_custom_call" | custom-call | bytes 12582912 | tf_op jit(solution)/shard_map/stage/pallas_call | solution.py:126
  15.1 0.0 collective-permute-done.1.got_ref
  15.2 1.6 %collective-permute-start.2 = (bf16[32,3200]{1,0:T(8,128)(2,1)S(1)}, bf16[32,3200]{1,0:T(8,128)(2,1)S(1)}, u32[]{:S(2)}, u32[]{:S(2)}) collective-permute-start(bf16[32,3200]{1,0:T(8,128)(2,1)S(1)} %join.5.source_ref), channel_id=1, source_target_pairs={{0,2},{1,3},{2,0},{3,1},{4,6},{5,7},{6,4},{7,5},{8,10},{9,11},{10,... | collective-permute-start | bytes 614408 | tf_op jit(solution)/shard_map/ppermute | solution.py:427
  16.8 0.3 select.6.after_ref.own_ref
  17.0 1.6 %collective-permute-start.3 = (bf16[16,3200]{1,0:T(8,128)(2,1)S(1)}, bf16[16,3200]{1,0:T(8,128)(2,1)S(1)}, u32[]{:S(2)}, u32[]{:S(2)}) collective-permute-start(bf16[16,3200]{1,0:T(8,128)(2,1)S(1)} %select.6.after_ref.own_ref), channel_id=1, source_target_pairs={{0,16},{1,17},{2,18},{3,19},{4,20},{5,21},{6,22},{7,23},{8,24},{9,... | collective-permute-start | bytes 307208 | tf_op jit(solution)/shard_map/ppermute | solution.py:427
  18.6 0.6 %plan.1 = (bf16[128,128]{1,0:T(8,128)(2,1)S(1)}, bf16[8,128]{1,0:T(8,128)(2,1)S(1)}, bf16[8,128]{1,0:T(8,128)(2,1)S(1)}, bf16[8,128]{1,0:T(8,128)(2,1)S(1)}, bf16[8,128]{1,0:T(8,128)(2,1)S(1)}) custom-call(s32[3]{0:T(128)S(1)} %pad_add_fusion.position_ref.refs_0_, s32[2,8]{1,0:T(2,128)S(1)} %bitcast.24, bf16[16,3200]{1,0:T(8,128)(2,1)S(1)} %select.6.after_ref.own_ref), custom_call_target="tpu_custom_call" | custom-call | tf_op jit(solution)/shard_map/plan/pallas_call | solution.py:468
  19.2 2.3 %collective-permute-done.2.source_ref = bf16[32,3200]{1,0:T(8,128)(2,1)S(1)} collective-permute-done((bf16[32,3200]{1,0:T(8,128)(2,1)S(1)}, bf16[32,3200]{1,0:T(8,128)(2,1)S(1)}, u32[]{:S(2)}, u32[]{:S(2)}) %collective-permute-start.2) | collective-permute-done | bytes 204832 | tf_op jit(solution)/shard_map/ppermute | solution.py:427
  21.5 0.3 select.7.got_ref
  21.8 0.0 collective-permute-done.3.refs_0_.own_ref
  21.8 0.1 collective-permute-start.4
  21.9 1.6 %collective-permute-start.5 = (bf16[16,3200]{1,0:T(8,128)(2,1)S(1)}, bf16[16,3200]{1,0:T(8,128)(2,1)S(1)}, u32[]{:S(2)}, u32[]{:S(2)}) collective-permute-start(bf16[16,3200]{1,0:T(8,128)(2,1)S(1)} %select.7.got_ref), channel_id=1, source_target_pairs={{0,16},{1,17},{2,18},{3,19},{4,20},{5,21},{6,22},{7,23},{8,24},{9,... | collective-permute-start | bytes 307208 | tf_op jit(solution)/shard_map/ppermute | solution.py:427
  23.4 0.0 collective-permute-done.4.refs_1_
  23.5 4.4 %first.1 = (f32[64,2048]{1,0:T(8,128)S(1)}, f32[64,2048]{1,0:T(8,128)S(1)}, f32[1024,128]{1,0:T(8,128)S(1)}) custom-call(s32[3]{0:T(128)S(1)} %pad_add_fusion.position_ref.refs_0_, bf16[32,3200]{1,0:T(8,128)(2,1)S(1)} %join.6.refs_0_, bf16[32,3200]{1,0:T(8,128)(2,1)S(1)} %collective-permute-done.4.refs_1_, ...), custom_call_target="tpu_custom_call" | custom-call | flops 402653184 | bytes 1572864 | tf_op jit(solution)/shard_map/first/pallas_call | solution.py:486
  27.9 0.0 collective-permute-done.5.got_ref
  27.9 0.2 collective-permute-start.6
  28.1 1.3 %collective-permute-done.6.refs_3_ = bf16[32,3200]{1,0:T(8,128)(2,1)S(1)} collective-permute-done((bf16[32,3200]{1,0:T(8,128)(2,1)S(1)}, bf16[32,3200]{1,0:T(8,128)(2,1)S(1)}, u32[]{:S(2)}, u32[]{:S(2)}) %collective-permute-start.6) | collective-permute-done | bytes 204832 | tf_op jit(solution)/shard_map/ppermute | solution.py:427
  29.4 4.9 %second.1 = (bf16[64,2048]{1,0:T(8,128)(2,1)S(1)}, bf16[64,2048]{1,0:T(8,128)(2,1)S(1)}, bf16[64,2048]{1,0:T(8,128)(2,1)S(1)}, bf16[64,3072]{1,0:T(8,128)(2,1)S(...) custom-call(s32[3]{0:T(128)S(1)} %pad_add_fusion.position_ref.refs_0_, bf16[32,3200]{1,0:T(8,128)(2,1)S(1)} %join.6.refs_0_, ...), custom_call_target="tpu_custom_call" | custom-call | flops 4831838208 | bytes 18874368 | tf_op jit(solution)/shard_map/second/pallas_call | solution.py:501
  34.3 3.9 %back_other.1 = bf16[784,128]{1,0:T(8,128)(2,1)S(1)} custom-call(s32[3]{0:T(128)S(1)} %pad_add_fusion.position_ref.refs_0_, bf16[64,2048]{1,0:T(8,128)(2,1)S(1)} %get-tuple-element.38.right.refs_0_, bf16[64,2048]{1,0:T(8,128)(2,1)S(1)} %get-tuple-element.39.grad_up.refs_1_.refs_2_, bf16[1536,2048]{1,0:T(8,128)(2,1)S(1)} %get-tuple-element.34.refs_4_.refs_2_, ...), custom_call_target="tpu_custom_call" | custom-call | flops 3221225472 | bytes 12582912 | tf_op jit(solution)/shard_map/back_other/pallas_call | solution.py:515
  38.2 1.5 %collective-permute-start.7 = (bf16[784,128]{1,0:T(8,128)(2,1)S(1)}, bf16[784,128]{1,0:T(8,128)(2,1)S(1)}, u32[]{:S(2)}, u32[]{:S(2)}) collective-permute-start(bf16[784,128]{1,0:T(8,128)(2,1)S(1)} %back_other.1), channel_id=1, source_target_pairs={{0,16},{1,17},{2,18},{3,19},{4,20},{5,21},{6,22},{7,23},{8,24},{9,... | collective-permute-start | bytes 602120 | tf_op jit(solution)/shard_map/ppermute | solution.py:427
  39.7 7.8 %gate_grad.1 = (bf16[3072,2048]{1,0:T(8,128)(2,1)}, f32[768,128]{1,0:T(8,128)S(1)}) custom-call(s32[3]{0:T(128)S(1)} %pad_add_fusion.position_ref.refs_0_, bf16[64,3072]{1,0:T(8,128)(2,1)S(1)} %get-tuple-element.37.left.refs_0_, bf16[64,2048]{1,0:T(8,128)(2,1)S(1)} %get-tuple-element.38.right.refs_0_, ...), custom_call_target="tpu_custom_call" | custom-call | flops 3221225472 | bytes 12582912 | tf_op jit(solution)/shard_map/gate_grad/pallas_call | solution.py:527
  47.5 1.0 %merge.1 = bf16[128,896]{1,0:T(8,128)(2,1)} custom-call(bf16[128,128]{1,0:T(8,128)(2,1)S(1)} %get-tuple-element.31.refs_0_.order_ref, f32[768,128]{1,0:T(8,128)S(1)} %get-tuple-element.41.own_ref, f32[1,64]{1,0:T(1,128)S(1)} %get-tuple-element.40.score_ref.refs_4_.routing_ref, bf16[784,128]{1,0:T(8,128)(2,1)S(1)} %collective-permute-done.7.refs_0_), custom_call_target="tpu_custom_call" | custom-call | tf_op jit(solution)/shard_map/merge/pallas_call | solution.py:537
  48.5 3.6 %all-to-all-start = ((bf16[16,8,896]{2,1,0:T(8,128)(2,1)}), bf16[16,8,896]{2,1,0:T(8,128)(2,1)S(1)}, u32[]{:S(2)}, u32[]{:S(2)}) async-start(bf16[16,8,896]{2,1,0:T(8,128)(2,1)} %bitcast.8), calls=%async_computation | async-start | bytes 458752 | tf_op jit(solution)/shard_map/all_to_all | solution.py:545
  52.1 9.3 %other_grads.1 = (bf16[3072,2048]{1,0:T(8,128)(2,1)}, bf16[2048,3072]{1,0:T(8,128)(2,1)}) custom-call(bf16[64,3072]{1,0:T(8,128)(2,1)S(1)} %get-tuple-element.37.left.refs_0_, bf16[64,2048]{1,0:T(8,128)(2,1)S(1)} %get-tuple-element.49.refs_1_, bf16[64,2048]{1,0:T(8,128)(2,1)S(1)} %get-tuple-element.39.grad_up.refs_1_.refs_2_, ...), custom_call_target="tpu_custom_call" | custom-call | flops 6442450944 | bytes 25165824 | tf_op jit(solution)/shard_map/other_grads/pallas_call | solution.py:398
  61.4 0.2 all-to-all-done
  61.6 0.8 %finish.1 = (bf16[8,1536]{1,0:T(8,128)(2,1)}, f32[2,8]{1,0:T(2,128)}) custom-call(bf16[128,896]{1,0:T(8,128)(2,1)S(1)} %bitcast.22, bf16[8,128]{1,0:T(8,128)(2,1)S(1)} %get-tuple-element.42.low_ref, bf16[8,128]{1,0:T(8,128)(2,1)S(1)} %get-tuple-element.43.high_ref, bf16[8,128]{1,0:T(8,128)(2,1)S(1)} %get-tuple-element.44.first_ref, ...), custom_call_target="tpu_custom_call" | custom-call | tf_op jit(solution)/shard_map/finish/pallas_call | solution.py:547
  (15 shorter events, 0.1 us)
Async XLA Ops:
  1.5 7.8 %collective-permute-start = (bf16[8,3200]{1,0:T(8,128)(2,1)S(1)}, bf16[8,3200]{1,0:T(8,128)(2,1)S(1)}, u32[]{:S(2)}, u32[]{:S(2)}) collective-permute-start(bf16[8,3200]{1,0:T(8,128)(2,1)S(1)} %pack.1.after_ref.own_ref), channel_id=1, source_target_pairs={{0,8},{1,9},{2,10},{3,11},{4,12},{5,13},{6,14},{7,15},{8,0},{9,1},... | collective-permute-start | bytes 153608 | tf_op jit(solution)/shard_map/ppermute | solution.py:427
  5.6 13.0 %copy-start.1 = (s32[8,2]{0,1:T(2,128)S(1)}, s32[8,2]{0,1:T(2,128)}, u32[]{:S(2)}) copy-start(s32[8,2]{0,1:T(2,128)} %param.10) | copy-start | bytes 196
  5.6 17.8 %slice-start = ((s8[12582912]{0:T(1024)(128)(4,1)}), s8[4194304]{0:T(1024)(128)(4,1)S(1)}, s32[]{:S(2)}) async-start(s8[12582912]{0:T(1024)(128)(4,1)} %bitcast.14), calls=%async_computation.1 | async-start | bytes 8388608
  5.6 17.8 %slice-start.1 = ((s8[12582912]{0:T(1024)(128)(4,1)}), s8[4194304]{0:T(1024)(128)(4,1)S(1)}, s32[]{:S(2)}) async-start(s8[12582912]{0:T(1024)(128)(4,1)} %bitcast.14), calls=%async_computation.2 | async-start | bytes 8388608
  5.6 17.8 %copy-start = (bf16[1,2048,3072]{2,1,0:T(8,128)(2,1)S(1)}, bf16[1,2048,3072]{2,1,0:T(8,128)(2,1)}, u32[]{:S(2)}) copy-start(bf16[1,2048,3072]{2,1,0:T(8,128)(2,1)} %param.13) | copy-start | bytes 37748740
  9.3 14.2 %slice-start.2 = ((s8[12582912]{0:T(1024)(128)(4,1)}), s8[4194304]{0:T(1024)(128)(4,1)S(1)}, s32[]{:S(2)}) async-start(s8[12582912]{0:T(1024)(128)(4,1)} %bitcast.14), calls=%async_computation.3 | async-start | bytes 8388608
  9.3 5.8 %collective-permute-start.1 = (bf16[16,3200]{1,0:T(8,128)(2,1)S(1)}, bf16[16,3200]{1,0:T(8,128)(2,1)S(1)}, u32[]{:S(2)}, u32[]{:S(2)}) collective-permute-start(bf16[16,3200]{1,0:T(8,128)(2,1)S(1)} %join.4.after_ref.own_ref), channel_id=1, source_target_pairs={{0,4},{1,5},{2,6},{3,7},{4,0},{5,1},{6,2},{7,3},{8,12},{9,13},{10,... | collective-permute-start | bytes 307208 | tf_op jit(solution)/shard_map/ppermute | solution.py:427
  15.2 6.3 %collective-permute-start.2 = (bf16[32,3200]{1,0:T(8,128)(2,1)S(1)}, bf16[32,3200]{1,0:T(8,128)(2,1)S(1)}, u32[]{:S(2)}, u32[]{:S(2)}) collective-permute-start(bf16[32,3200]{1,0:T(8,128)(2,1)S(1)} %join.5.source_ref), channel_id=1, source_target_pairs={{0,2},{1,3},{2,0},{3,1},{4,6},{5,7},{6,4},{7,5},{8,10},{9,11},{10,... | collective-permute-start | bytes 614408 | tf_op jit(solution)/shard_map/ppermute | solution.py:427
  17.0 4.7 %collective-permute-start.3 = (bf16[16,3200]{1,0:T(8,128)(2,1)S(1)}, bf16[16,3200]{1,0:T(8,128)(2,1)S(1)}, u32[]{:S(2)}, u32[]{:S(2)}) collective-permute-start(bf16[16,3200]{1,0:T(8,128)(2,1)S(1)} %select.6.after_ref.own_ref), channel_id=1, source_target_pairs={{0,16},{1,17},{2,18},{3,19},{4,20},{5,21},{6,22},{7,23},{8,24},{9,... | collective-permute-start | bytes 307208 | tf_op jit(solution)/shard_map/ppermute | solution.py:427
  21.8 1.6 %collective-permute-start.4 = (bf16[32,3200]{1,0:T(8,128)(2,1)S(1)}, bf16[32,3200]{1,0:T(8,128)(2,1)S(1)}, u32[]{:S(2)}, u32[]{:S(2)}) collective-permute-start(bf16[32,3200]{1,0:T(8,128)(2,1)S(1)} %join.6.refs_0_), channel_id=1, source_target_pairs={{0,1},{1,0},{2,3},{3,2},{4,5},{5,4},{6,7},{7,6},{8,9},{9,8},{10,11... | collective-permute-start | bytes 614408 | tf_op jit(solution)/shard_map/ppermute | solution.py:427
  21.9 6.0 %collective-permute-start.5 = (bf16[16,3200]{1,0:T(8,128)(2,1)S(1)}, bf16[16,3200]{1,0:T(8,128)(2,1)S(1)}, u32[]{:S(2)}, u32[]{:S(2)}) collective-permute-start(bf16[16,3200]{1,0:T(8,128)(2,1)S(1)} %select.7.got_ref), channel_id=1, source_target_pairs={{0,16},{1,17},{2,18},{3,19},{4,20},{5,21},{6,22},{7,23},{8,24},{9,... | collective-permute-start | bytes 307208 | tf_op jit(solution)/shard_map/ppermute | solution.py:427
  27.9 1.5 %collective-permute-start.6 = (bf16[32,3200]{1,0:T(8,128)(2,1)S(1)}, bf16[32,3200]{1,0:T(8,128)(2,1)S(1)}, u32[]{:S(2)}, u32[]{:S(2)}) collective-permute-start(bf16[32,3200]{1,0:T(8,128)(2,1)S(1)} %join.7.refs_2_), channel_id=1, source_target_pairs={{0,1},{1,0},{2,3},{3,2},{4,5},{5,4},{6,7},{7,6},{8,9},{9,8},{10,11... | collective-permute-start | bytes 614408 | tf_op jit(solution)/shard_map/ppermute | solution.py:427
  38.2 9.2 %collective-permute-start.7 = (bf16[784,128]{1,0:T(8,128)(2,1)S(1)}, bf16[784,128]{1,0:T(8,128)(2,1)S(1)}, u32[]{:S(2)}, u32[]{:S(2)}) collective-permute-start(bf16[784,128]{1,0:T(8,128)(2,1)S(1)} %back_other.1), channel_id=1, source_target_pairs={{0,16},{1,17},{2,18},{3,19},{4,20},{5,21},{6,22},{7,23},{8,24},{9,... | collective-permute-start | bytes 602120 | tf_op jit(solution)/shard_map/ppermute | solution.py:427
  48.5 13.1 %all-to-all-start = ((bf16[16,8,896]{2,1,0:T(8,128)(2,1)}), bf16[16,8,896]{2,1,0:T(8,128)(2,1)S(1)}, u32[]{:S(2)}, u32[]{:S(2)}) async-start(bf16[16,8,896]{2,1,0:T(8,128)(2,1)} %bitcast.8), calls=%async_computation | async-start | bytes 458752 | tf_op jit(solution)/shard_map/all_to_all | solution.py:545

commit v4 on v3

--- a/solution.py
+++ b/solution.py
@@ -84,35 +84,18 @@
     copies[3].wait()
 
 
-def part_copies(position, by_row, masks, source, target, sems):
+def part_copies(position, masks, width, offset, source, target, sems):
+    rows = target.shape[0] // len(masks)
     copies = []
     for i, mask in enumerate(masks):
-        if by_row:
-            width = target.shape[0] // len(masks)
-            place = pl.ds(pl.multiple_of((position ^ mask) * width, width), width)
-            pair = (source.at[place], target.at[pl.ds(i * width, width)])
-        else:
-            width = target.shape[1]
-            depth = target.shape[0] // len(masks)
-            place = pl.ds(pl.multiple_of((position ^ mask) * width, width), width)
-            pair = (source.at[:, place], target.at[pl.ds(i * depth, depth)])
-        copies.append(pltpu.make_async_copy(*pair, sems.at[i]))
+        start = pl.multiple_of((position ^ mask) * width + offset, rows)
+        place = target.at[pl.ds(i * rows, rows)]
+        copies.append(pltpu.make_async_copy(source.at[pl.ds(start, rows)], place, sems.at[i]))
     return copies
 
 
-def part_shape(weight, by_row, masks, width):
-    if by_row:
-        return pltpu.VMEM((width * len(masks), weight.shape[1]), BF)
-    return pltpu.VMEM((weight.shape[0] * len(masks), width), BF)
-
-
-def stage_kernel(jobs, position_ref, after_ref, *refs):
-    count = len(jobs)
-    sources, outs = refs[:count], refs[count : 2 * count]
-    token_ref = refs[2 * count]
-    copies = []
-    for (by_row, masks), source, out, sems in zip(jobs, sources, outs, refs[2 * count + 1 :]):
-        copies += part_copies(position_ref[0], by_row, masks, source, out, sems)
+def stage_kernel(masks, width, offset, position_ref, after_ref, source_ref, out_ref, token_ref, sems):
+    copies = part_copies(position_ref[0], masks, width, offset, source_ref, out_ref, sems)
     for copy in copies:
         copy.start()
     token_ref[...] = jnp.zeros_like(token_ref)
@@ -120,20 +103,18 @@
         copy.wait()
 
 
-def stage(position, jobs, width, after):
-    outs = [part_shape(*job, width) for job in jobs]
-    size = sum(out.shape[0] * out.shape[1] for out in outs)
-    *kept, token = pl.pallas_call(
-        functools.partial(stage_kernel, [job[1:] for job in jobs]),
-        out_shape=outs + [pltpu.VMEM((8, LANES), F32)],
-        in_specs=[SMEM, ANY] + [ANY] * len(jobs),
-        out_specs=[ANY] * len(jobs) + [VMEM],
-        scratch_shapes=[pltpu.SemaphoreType.DMA((len(job[2]),)) for job in jobs],
+def stage(position, weight, masks, width, offset, rows, after):
+    columns = weight.shape[1]
+    return pl.pallas_call(
+        functools.partial(stage_kernel, masks, width, offset),
+        out_shape=[pltpu.VMEM((rows * len(masks), columns), BF), pltpu.VMEM((8, LANES), F32)],
+        in_specs=[SMEM, ANY, ANY],
+        out_specs=[ANY, VMEM],
+        scratch_shapes=[pltpu.SemaphoreType.DMA((len(masks),))],
         compiler_params=params(2),
-        cost_estimate=cost(0, 4 * size),
+        cost_estimate=cost(0, 4 * rows * len(masks) * columns),
         name="stage",
-    )(position, after, *[pltpu.with_memory_space_constraint(job[0], pltpu.HBM) for job in jobs])
-    return kept, token
+    )(position, after, pltpu.with_memory_space_constraint(weight, pltpu.HBM))
 
 
 def join_kernel(own_ref, got_ref, *refs):
@@ -168,15 +149,15 @@
     out_ref[...] = dot(jnp.where(take, 1.0, 0.0).astype(BF), source_ref[...], 0, 0).astype(BF)
 
 
-def select(expert, source, blocks, after):
+def select(expert, source, blocks, *after):
     return pl.pallas_call(
         select_kernel,
         out_shape=pltpu.VMEM((blocks * CAP, source.shape[1]), BF),
-        in_specs=[SMEM, VMEM, ANY],
+        in_specs=[SMEM, VMEM] + [ANY] * len(after),
         out_specs=VMEM,
         compiler_params=params(4),
         name="select",
-    )(expert, source, after)
+    )(expert, source, *after)
 
 
 def stacked(refs, start, size):
@@ -209,18 +190,18 @@
         up_out[:, units] = dot(inputs, w_up[here, units], 1, 0)
 
 
-def second_kernel(count, others, position_ref, *refs):
+def second_kernel(count, others, position_ref, after_ref, *refs):
     own = refs[:count]
     parts = [refs[count * (m + 1) : count * (m + 2)] for m in range(others)]
     rest = refs[count * (others + 1) :]
-    w_gate, w_up, w_down, gate_in, up_in, through_in = rest[:6]
-    weighted_ref, grad_gate_ref, grad_up_ref, inputs_ref, upstream_ref, routing_ref = rest[6:12]
-    through_ref = rest[12]
+    w_low, w_high, w_up, w_down, gate_in, up_in, through_in = rest[:7]
+    weighted_ref, grad_gate_ref, grad_up_ref, inputs_ref, upstream_ref, routing_ref = rest[7:13]
+    through_ref = rest[13]
     full = own[0].shape[1]
     width = (full - LANES) // 2
     position, expert = position_ref[0], position_ref[1]
     places = [pl.ds(pl.multiple_of((position ^ m) * width, width), width) for m in range(others + 1)]
-    hidden = w_gate.shape[1]
+    hidden = w_up.shape[1]
     slots = gate_in.shape[0]
     half = hidden // 2
     tile = min(512, half)
@@ -236,11 +217,12 @@
         inputs_ref[:, places[m]] = stacked(blocks, 0, width)
         upstream_ref[:, places[m]] = stacked(blocks, width, width)
     xs = [stacked(part, 0, width) for part in parts]
-    x = jnp.concatenate(xs, axis=1)
+    low = jnp.concatenate([x[:, : width // 2] for x in xs], axis=1)
+    high = jnp.concatenate([x[:, width // 2 :] for x in xs], axis=1)
     score = jnp.zeros((slots, 1), F32)
     for start in range(0, hidden, tile):
         units = slice(start, start + tile)
-        pre_gate = gate_in[:, units] + dot(x, w_gate[:, units], 1, 0)
+        pre_gate = gate_in[:, units] + dot(low, w_low[:, units], 1, 0) + dot(high, w_high[:, units], 1, 0)
         pre_up = up_in[:, units]
         for m in range(others):
             pre_up = pre_up + dot(xs[m], w_up[places[m + 1], units], 1, 0)
@@ -267,26 +249,26 @@
     return jnp.where(sub == 0, jnp.broadcast_to(wide, sub.shape), 0.0).astype(BF)
 
 
-def back(position, mask, grad_gate, grad_up, w_gate, w_up, routing_ref, out_ref):
-    width = w_gate.shape[0]
-    half = width // 2
-
-    gate_rows, up_rows = low_high(grad_gate[...]), low_high(grad_up[...])
-
+def back(position, mask, grad_gate, grad_up, w_low, w_high, w_up, routing_ref, out_ref):
+    half = w_low.shape[0]
+    width = 2 * half
+    low, high = low_high(grad_gate[...])
     rows = pl.ds(pl.multiple_of((position ^ mask) * width, width), width)
-    part = folded(w_gate, *gate_rows) + folded(w_up.at[rows], *up_rows)
+    part = dot(w_low[...], low, 1, 1) + dot(w_high[...], high, 1, 1)
+    part = part + folded(w_up.at[rows], *low_high(grad_up[...]))
     out_ref[:half, :] = part.astype(out_ref.dtype)
     if out_ref.shape[0] > half:
         out_ref[half:, :] = halves(routing_ref[...], out_ref.shape[0] - half)
 
 
 def back_other_kernel(others, position_ref, *refs):
-    grad_gate, grad_up, w_gate, w_up, routing_ref = refs[:5]
-    outs = refs[5:]
-    width = w_gate.shape[0] // others
+    grad_gate, grad_up, w_low, w_high, w_up, routing_ref = refs[:6]
+    outs = refs[6:]
+    half = w_low.shape[0] // others
     for m, out_ref in enumerate(outs):
-        rows = pl.ds(m * width, width)
-        back(position_ref[0], m + 1, grad_gate, grad_up, w_gate.at[rows], w_up, routing_ref, out_ref)
+        rows = pl.ds(m * half, half)
+        weights = w_low.at[rows], w_high.at[rows], w_up
+        back(position_ref[0], m + 1, grad_gate, grad_up, *weights, routing_ref, out_ref)
 
 
 def merge_kernel(order_ref, own_ref, routing_ref, *refs):
@@ -351,7 +333,9 @@
 
 def outer_back_kernel(tile, depth, position_ref, left, right, grad_up, w_gate, w_up, score_ref, out, kept, *scratch):
     pending = outer_copies(tile, depth, [left], [right], [out], *scratch)
-    back(position_ref[0], 0, right, grad_up, w_gate, w_up, score_ref, kept)
+    half = w_gate.shape[0] // 2
+    weights = w_gate.at[pl.ds(0, half)], w_gate.at[pl.ds(half, half)], w_up
+    back(position_ref[0], 0, right, grad_up, *weights, score_ref, kept)
     for copy in pending:
         copy.wait()
 
@@ -448,36 +432,26 @@
 
     gate = w_gate[0]
     up, down = [pltpu.with_memory_space_constraint(w[0], pltpu.VMEM) for w in (w_up, w_down)]
-    plan = [[(gate, True, own)], [(gate, True, rest)]]
+    half = width // 2
+    plan = [(own, 0, width), (rest, 0, half), (rest, half, half)]
     staged = []
     offsets = [0]
     mask = n_wide // 2
     while mask >= replicas:
         last = mask == replicas
         got = swap(gathered, mask, 0)
-        jobs = sum(plan if last else plan[:1], [])
-        plan = plan[1:]
-        if jobs:
-            kept, token = stage(position, jobs, width, gathered)
-            staged += kept
+        masks, offset, rows = plan.pop(0)
+        kept, token = stage(position, gate, masks, width, offset, rows, gathered)
+        staged.append(kept)
         if not last:
-            gathered = join(gathered, got, token if jobs else got)
+            gathered = join(gathered, got, token)
         else:
-            early = select(expert, gathered, len(offsets), position)
-            every = offsets + [offset ^ mask for offset in offsets]
-            order, *hits = pl.pallas_call(
-                functools.partial(plan_kernel, replicas, every),
-                out_shape=[pltpu.VMEM((2 * slots, 2 * slots), BF)] + [pltpu.VMEM((tok, 2 * slots), BF)] * 4,
-                in_specs=[SMEM, VMEM, ANY],
-                out_specs=[VMEM] * 5,
-                compiler_params=params(4),
-                name="plan",
-            )(position, experts_t, early)
-            late = select(expert, got, len(offsets), order)
+            early = select(expert, gathered, len(offsets))
+            late = select(expert, got, len(offsets), token)
         offsets = offsets + [offset ^ mask for offset in offsets]
         mask //= 2
 
-    wg_own, wg_rest = staged
+    wg_own, wg_low, wg_high = staged
     away = [[swap(early, 0, m), swap(late, 0, m)] for m in rest]
     chosen = join(early, late, away[0][0])
     near = [chosen] + [swap(chosen, r, 0) for r in range(1, replicas)]
@@ -493,6 +467,14 @@
         name="first",
     )(position, *near, wg_own, up, down)
 
+    order, *hits = pl.pallas_call(
+        functools.partial(plan_kernel, replicas, offsets),
+        out_shape=[pltpu.VMEM((2 * slots, 2 * slots), BF)] + [pltpu.VMEM((tok, 2 * slots), BF)] * 4,
+        in_specs=[SMEM, VMEM, ANY],
+        out_specs=[VMEM] * 5,
+        compiler_params=params(4),
+        name="plan",
+    )(position, experts_t, partial[0])
     parts = []
     for early_part, late_part in away:
         part = join(early_part, late_part, partial[0])
@@ -503,24 +485,24 @@
         out_shape=[shape(slots, hidden)] * 3
         + [shape(slots, width * n_tensor)] * 2
         + [shape(1, slots, F32)],
-        in_specs=[SMEM] + [VMEM] * (count * n_tensor + 6),
+        in_specs=[SMEM, ANY] + [VMEM] * (count * n_tensor + 7),
         out_specs=[VMEM] * 6,
         scratch_shapes=[pltpu.VMEM((2 * slots, hidden // 2), F32)],
         compiler_params=params(6),
         cost_estimate=cost(24 * slots * width * hidden, 6 * width * hidden),
         name="second",
-    )(position, *near, *sum(parts, []), wg_rest, up, down, *partial)
+    )(position, order, *near, *sum(parts, []), wg_low, wg_high, up, down, *partial)
 
     half = width // 2
     sent = pl.pallas_call(
         functools.partial(back_other_kernel, others),
         out_shape=[shape(half + 16, 2 * slots)] * others,
-        in_specs=[SMEM] + [VMEM] * 5,
+        in_specs=[SMEM] + [VMEM] * 6,
         out_specs=[VMEM] * others,
         compiler_params=params(5),
         cost_estimate=cost(16 * slots * width * hidden, 4 * width * hidden),
         name="back_other",
-    )(position, grad_gate, grad_up, wg_rest, up, score)
+    )(position, grad_gate, grad_up, wg_low, wg_high, up, score)
     returned = [swap(value, 0, m) for m, value in zip(rest, sent)]
     grad_shape = (inputs.shape[1], hidden)
     tile, depth, scratch = outer_plan([grad_shape], slots)

time: 62.7 us -> 62.6 us (level)
  waiting for transfers between devices: 3.78 us -> 1.31 us
  Pallas kernels: 41.9 us -> 43.1 us
  starting transfers between devices: 15.8 us -> 16.9 us
    ppermute x8, waiting for transfers between devices: 3.56 us -> 1.08 us  [swap(): return lax.ppermute(value, axes, pairs)]
    pallas_call x3 -> x4, Pallas kernels: 8.41 us -> 9.63 us  [the longest x3 9 us: stage(): pl.pallas_call(functools.partial(stage_kernel, masks, width, offset), out...]
    all_to_all x1, starting transfers between devices: 3.56 us -> 4.69 us  [shards(): lax.all_to_all(merged, 'wide', split_axis=0, concat_axis=0, tiled=True)]
  transfers between devices with their start and end apart: 9 -> 9, of which waited for: 3 -> 3; matrix products, arithmetic and copies ran while one was open for 0% -> 0% of each run, Pallas kernels for 49% -> 51%
where the time goes in v4:
time: 62.6 us; the launch traced here: 62.3 us
  Pallas kernels  43.1 us (69%)
  starting transfers between devices  16.9 us (27%)
  waiting for transfers between devices  1.31 us (2%)
  between operations  0.87 us (1%)
    ppermute x8, starting transfers between devices, swap(): return lax.ppermute(value, axes, pairs)  12.2 us
    pallas_call x1, Pallas kernels, outer(): pl.pallas_call(functools.partial(outer_kernel, tile, depth, len(pairs)),...  9.29 us
    pallas_call x3, Pallas kernels, stage(): pl.pallas_call(functools.partial(stage_kernel, masks, width, offset), out...  9 us
    pallas_call x1, Pallas kernels, shards(): pl.pallas_call(functools.partial(outer_back_kernel, tile, depth), out_sha...  7.79 us
    pallas_call x1, Pallas kernels, shards(): pl.pallas_call(functools.partial(second_kernel, count, others), out_shape...  4.82 us
    all_to_all x1, starting transfers between devices, shards(): lax.all_to_all(merged, 'wide', split_axis=0, concat_axis=0, tiled=True)  4.69 us
    pallas_call x1, Pallas kernels, shards(): pl.pallas_call(functools.partial(first_kernel, len(near)), out_shape=[sha...  4.39 us
    pallas_call x1, Pallas kernels, shards(): pl.pallas_call(functools.partial(back_other_kernel, others), out_shape=[s...  3.94 us
  transfers between devices with their start and end apart: 9, of which 3 were waited for; matrix products, arithmetic and copies ran while one was open for 0% of the time, Pallas kernels for 51%

profile of v4, /device:TPU:0, one launch (start us, length us, event | category | flops | bytes accessed | tf_op | source)
XLA Modules:
  0.0 62.3 jit_solution(13131015692953405430)
XLA Ops:
  0.6 0.8 %pack.1.after_ref.own_ref = bf16[8,3200]{1,0:T(8,128)(2,1)S(1)} custom-call(bf16[8,1536]{1,0:T(8,128)(2,1)} %tokens_hbm.1, bf16[8,1536]{1,0:T(8,128)(2,1)} %cotangent_hbm.1, bf16[2,8]{1,0:T(2,128)(2,1)} %bitcast.28, s32[2,8]{1,0:T(2,128)} %bitcast.23), custom_call_target="tpu_custom_call" | custom-call | tf_op jit(solution)/shard_map/pack/pallas_call | solution.py:419
  1.5 4.1 %collective-permute-start = (bf16[8,3200]{1,0:T(8,128)(2,1)S(1)}, bf16[8,3200]{1,0:T(8,128)(2,1)S(1)}, u32[]{:S(2)}, u32[]{:S(2)}) collective-permute-start(bf16[8,3200]{1,0:T(8,128)(2,1)S(1)} %pack.1.after_ref.own_ref), channel_id=1, source_target_pairs={{0,8},{1,9},{2,10},{3,11},{4,12},{5,13},{6,14},{7,15},{8,0},{9,1},... | collective-permute-start | bytes 153608 | tf_op jit(solution)/shard_map/ppermute | solution.py:411
  5.6 0.1 pad_add_fusion.position_ref
  5.6 3.3 %stage.3 = (bf16[1536,2048]{1,0:T(8,128)(2,1)S(1)}, f32[8,128]{1,0:T(8,128)S(1)}) custom-call(s32[3]{0:T(128)S(1)} %pad_add_fusion.position_ref, bf16[8,3200]{1,0:T(8,128)(2,1)S(1)} %pack.1.after_ref.own_ref, bf16[3072,2048]{1,0:T(8,128)(2,1)} %bitcast.25), custom_call_target="tpu_custom_call" | custom-call | bytes 12582912 | tf_op jit(solution)/shard_map/stage/pallas_call | solution.py:108
  9.0 0.0 slice-start
  9.0 0.0 copy-start
  9.1 1.6 %collective-permute-start.1 = (bf16[16,3200]{1,0:T(8,128)(2,1)S(1)}, bf16[16,3200]{1,0:T(8,128)(2,1)S(1)}, u32[]{:S(2)}, u32[]{:S(2)}) collective-permute-start(bf16[16,3200]{1,0:T(8,128)(2,1)S(1)} %join.4.after_ref.own_ref), channel_id=1, source_target_pairs={{0,4},{1,5},{2,6},{3,7},{4,0},{5,1},{6,2},{7,3},{8,12},{9,13},{10,... | collective-permute-start | bytes 307208 | tf_op jit(solution)/shard_map/ppermute | solution.py:411
  10.7 3.2 %stage.4 = (bf16[768,2048]{1,0:T(8,128)(2,1)S(1)}, f32[8,128]{1,0:T(8,128)S(1)}) custom-call(s32[3]{0:T(128)S(1)} %pad_add_fusion.position_ref, bf16[16,3200]{1,0:T(8,128)(2,1)S(1)} %join.4.after_ref.own_ref, bf16[3072,2048]{1,0:T(8,128)(2,1)} %bitcast.26), custom_call_target="tpu_custom_call" | custom-call | bytes 6291456 | tf_op jit(solution)/shard_map/stage/pallas_call | solution.py:108
  14.0 1.6 %collective-permute-start.2 = (bf16[32,3200]{1,0:T(8,128)(2,1)S(1)}, bf16[32,3200]{1,0:T(8,128)(2,1)S(1)}, u32[]{:S(2)}, u32[]{:S(2)}) collective-permute-start(bf16[32,3200]{1,0:T(8,128)(2,1)S(1)} %join.5.source_ref.after_ref), channel_id=1, source_target_pairs={{0,2},{1,3},{2,0},{3,1},{4,6},{5,7},{6,4},{7,5},{8,10},{9,11},{10,... | collective-permute-start | bytes 614408 | tf_op jit(solution)/shard_map/ppermute | solution.py:411
  15.5 0.3 select.6.own_ref
  15.8 0.0 slice-start.2
  15.8 1.6 %collective-permute-start.3 = (bf16[16,3200]{1,0:T(8,128)(2,1)S(1)}, bf16[16,3200]{1,0:T(8,128)(2,1)S(1)}, u32[]{:S(2)}, u32[]{:S(2)}) collective-permute-start(bf16[16,3200]{1,0:T(8,128)(2,1)S(1)} %select.6.own_ref), channel_id=1, source_target_pairs={{0,16},{1,17},{2,18},{3,19},{4,20},{5,21},{6,22},{7,23},{8,24},{9,... | collective-permute-start | bytes 307208 | tf_op jit(solution)/shard_map/ppermute | solution.py:411
  17.4 2.4 %stage.5 = (bf16[768,2048]{1,0:T(8,128)(2,1)S(1)}, f32[8,128]{1,0:T(8,128)S(1)}) custom-call(s32[3]{0:T(128)S(1)} %pad_add_fusion.position_ref, bf16[32,3200]{1,0:T(8,128)(2,1)S(1)} %join.5.source_ref.after_ref, bf16[3072,2048]{1,0:T(8,128)(2,1)} %bitcast.27), custom_call_target="tpu_custom_call" | custom-call | bytes 6291456 | tf_op jit(solution)/shard_map/stage/pallas_call | solution.py:108
  19.8 0.4 collective-permute-done.2.source_ref
  20.3 0.3 select.7.got_ref
  20.6 0.0 collective-permute-done.3.refs_0_.own_ref
  20.6 0.1 collective-permute-start.4
  20.7 1.6 %collective-permute-start.5 = (bf16[16,3200]{1,0:T(8,128)(2,1)S(1)}, bf16[16,3200]{1,0:T(8,128)(2,1)S(1)}, u32[]{:S(2)}, u32[]{:S(2)}) collective-permute-start(bf16[16,3200]{1,0:T(8,128)(2,1)S(1)} %select.7.got_ref), channel_id=1, source_target_pairs={{0,16},{1,17},{2,18},{3,19},{4,20},{5,21},{6,22},{7,23},{8,24},{9,... | collective-permute-start | bytes 307208 | tf_op jit(solution)/shard_map/ppermute | solution.py:411
  22.3 0.0 copy-start.1
  22.3 4.4 %first.1 = (f32[64,2048]{1,0:T(8,128)S(1)}, f32[64,2048]{1,0:T(8,128)S(1)}, f32[1024,128]{1,0:T(8,128)S(1)}) custom-call(s32[3]{0:T(128)S(1)} %pad_add_fusion.position_ref, bf16[32,3200]{1,0:T(8,128)(2,1)S(1)} %join.6.refs_0_, bf16[32,3200]{1,0:T(8,128)(2,1)S(1)} %collective-permute-done.4.refs_1_, bf16[1536,2048]{1,0:T(8,128)(2,1)S(1)} %get-tuple-element.34.refs_2_.w_gate, ...), custom_call_target="tpu_custom_call" | custom-call | flops 402653184 | bytes 1572864 | tf_op jit(solution)/shard_map/first/pallas_call | solution.py:460
  26.7 0.2 collective-permute-start.6
  27.0 0.6 %plan.1 = (bf16[128,128]{1,0:T(8,128)(2,1)S(1)}, bf16[8,128]{1,0:T(8,128)(2,1)S(1)}, bf16[8,128]{1,0:T(8,128)(2,1)S(1)}, bf16[8,128]{1,0:T(8,128)(2,1)S(1)}, bf16[8,128]{1,0:T(8,128)(2,1)S(1)}) custom-call(s32[3]{0:T(128)S(1)} %pad_add_fusion.position_ref, s32[2,8]{1,0:T(2,128)S(1)} %bitcast.24, f32[64,2048]{1,0:T(8,128)S(1)} %get-tuple-element.35.after_ref.refs_0_.refs_8_), custom_call_target="tpu_custom_call" | custom-call | tf_op jit(solution)/shard_map/plan/pallas_call | solution.py:470
  27.6 0.6 %collective-permute-done.6.refs_3_ = bf16[32,3200]{1,0:T(8,128)(2,1)S(1)} collective-permute-done((bf16[32,3200]{1,0:T(8,128)(2,1)S(1)}, bf16[32,3200]{1,0:T(8,128)(2,1)S(1)}, u32[]{:S(2)}, u32[]{:S(2)}) %collective-permute-start.6) | collective-permute-done | bytes 204832 | tf_op jit(solution)/shard_map/ppermute | solution.py:411
  28.2 4.8 %second.1 = (bf16[64,2048]{1,0:T(8,128)(2,1)S(1)}, bf16[64,2048]{1,0:T(8,128)(2,1)S(1)}, bf16[64,2048]{1,0:T(8,128)(2,1)S(1)}, bf16[64,3072]{1,0:T(8,128)(2,1)S(...) custom-call(s32[3]{0:T(128)S(1)} %pad_add_fusion.position_ref, ...), custom_call_target="tpu_custom_call" | custom-call | flops 4831838208 | bytes 18874368 | tf_op jit(solution)/shard_map/second/pallas_call | solution.py:483
  33.1 3.9 %back_other.1 = bf16[784,128]{1,0:T(8,128)(2,1)S(1)} custom-call(s32[3]{0:T(128)S(1)} %pad_add_fusion.position_ref, bf16[64,2048]{1,0:T(8,128)(2,1)S(1)} %get-tuple-element.42.right.refs_0_, bf16[64,2048]{1,0:T(8,128)(2,1)S(1)} %get-tuple-element.43.grad_up.refs_1_.refs_2_, bf16[768,2048]{1,0:T(8,128)(2,1)S(1)} %get-tuple-element.37.refs_4_.refs_2_, ...), custom_call_target="tpu_custom_call" | custom-call | flops 3221225472 | bytes 12582912 | tf_op jit(solution)/shard_map/back_other/pallas_call | solution.py:497
  37.0 1.4 %collective-permute-start.7 = (bf16[784,128]{1,0:T(8,128)(2,1)S(1)}, bf16[784,128]{1,0:T(8,128)(2,1)S(1)}, u32[]{:S(2)}, u32[]{:S(2)}) collective-permute-start(bf16[784,128]{1,0:T(8,128)(2,1)S(1)} %back_other.1), channel_id=1, source_target_pairs={{0,16},{1,17},{2,18},{3,19},{4,20},{5,21},{6,22},{7,23},{8,24},{9,... | collective-permute-start | bytes 602120 | tf_op jit(solution)/shard_map/ppermute | solution.py:411
  38.5 7.8 %gate_grad.1 = (bf16[3072,2048]{1,0:T(8,128)(2,1)}, f32[768,128]{1,0:T(8,128)S(1)}) custom-call(s32[3]{0:T(128)S(1)} %pad_add_fusion.position_ref, bf16[64,3072]{1,0:T(8,128)(2,1)S(1)} %get-tuple-element.41.left.refs_0_, bf16[64,2048]{1,0:T(8,128)(2,1)S(1)} %get-tuple-element.42.right.refs_0_, ...), custom_call_target="tpu_custom_call" | custom-call | flops 3221225472 | bytes 12582912 | tf_op jit(solution)/shard_map/gate_grad/pallas_call | solution.py:509
  46.3 1.0 %merge.1 = bf16[128,896]{1,0:T(8,128)(2,1)} custom-call(bf16[128,128]{1,0:T(8,128)(2,1)S(1)} %get-tuple-element.36.after_ref.order_ref, f32[768,128]{1,0:T(8,128)S(1)} %get-tuple-element.45.own_ref, f32[1,64]{1,0:T(1,128)S(1)} %get-tuple-element.44.score_ref.refs_5_.routing_ref, bf16[784,128]{1,0:T(8,128)(2,1)S(1)} %collective-permute-done.7.refs_0_), custom_call_target="tpu_custom_call" | custom-call | tf_op jit(solution)/shard_map/merge/pallas_call | solution.py:519
  47.3 4.7 %all-to-all-start = ((bf16[16,8,896]{2,1,0:T(8,128)(2,1)}), bf16[16,8,896]{2,1,0:T(8,128)(2,1)S(1)}, u32[]{:S(2)}, u32[]{:S(2)}) async-start(bf16[16,8,896]{2,1,0:T(8,128)(2,1)} %bitcast.8), calls=%async_computation | async-start | bytes 458752 | tf_op jit(solution)/shard_map/all_to_all | solution.py:527
  52.0 9.3 %other_grads.1 = (bf16[3072,2048]{1,0:T(8,128)(2,1)}, bf16[2048,3072]{1,0:T(8,128)(2,1)}) custom-call(bf16[64,3072]{1,0:T(8,128)(2,1)S(1)} %get-tuple-element.41.left.refs_0_, bf16[64,2048]{1,0:T(8,128)(2,1)S(1)} %get-tuple-element.53.refs_1_, bf16[64,2048]{1,0:T(8,128)(2,1)S(1)} %get-tuple-element.43.grad_up.refs_1_.refs_2_, ...), custom_call_target="tpu_custom_call" | custom-call | flops 6442450944 | bytes 25165824 | tf_op jit(solution)/shard_map/other_grads/pallas_call | solution.py:382
  61.3 0.2 all-to-all-done
  61.5 0.8 %finish.1 = (bf16[8,1536]{1,0:T(8,128)(2,1)}, f32[2,8]{1,0:T(2,128)}) custom-call(bf16[128,896]{1,0:T(8,128)(2,1)S(1)} %bitcast.22, bf16[8,128]{1,0:T(8,128)(2,1)S(1)} %get-tuple-element.46.low_ref, bf16[8,128]{1,0:T(8,128)(2,1)S(1)} %get-tuple-element.47.high_ref, bf16[8,128]{1,0:T(8,128)(2,1)S(1)} %get-tuple-element.48.first_ref, ...), custom_call_target="tpu_custom_call" | custom-call | tf_op jit(solution)/shard_map/finish/pallas_call | solution.py:529
  (16 shorter events, 0.1 us)
Async XLA Ops:
  1.5 7.5 %collective-permute-start = (bf16[8,3200]{1,0:T(8,128)(2,1)S(1)}, bf16[8,3200]{1,0:T(8,128)(2,1)S(1)}, u32[]{:S(2)}, u32[]{:S(2)}) collective-permute-start(bf16[8,3200]{1,0:T(8,128)(2,1)S(1)} %pack.1.after_ref.own_ref), channel_id=1, source_target_pairs={{0,8},{1,9},{2,10},{3,11},{4,12},{5,13},{6,14},{7,15},{8,0},{9,1},... | collective-permute-start | bytes 153608 | tf_op jit(solution)/shard_map/ppermute | solution.py:411
  9.0 13.2 %slice-start = ((s8[12582912]{0:T(1024)(128)(4,1)}), s8[4194304]{0:T(1024)(128)(4,1)S(1)}, s32[]{:S(2)}) async-start(s8[12582912]{0:T(1024)(128)(4,1)} %bitcast.14), calls=%async_computation.1 | async-start | bytes 8388608
  9.0 13.2 %slice-start.1 = ((s8[12582912]{0:T(1024)(128)(4,1)}), s8[4194304]{0:T(1024)(128)(4,1)S(1)}, s32[]{:S(2)}) async-start(s8[12582912]{0:T(1024)(128)(4,1)} %bitcast.14), calls=%async_computation.2 | async-start | bytes 8388608
  9.0 13.2 %copy-start = (bf16[1,2048,3072]{2,1,0:T(8,128)(2,1)S(1)}, bf16[1,2048,3072]{2,1,0:T(8,128)(2,1)}, u32[]{:S(2)}) copy-start(bf16[1,2048,3072]{2,1,0:T(8,128)(2,1)} %param.13) | copy-start | bytes 37748740
  9.1 4.9 %collective-permute-start.1 = (bf16[16,3200]{1,0:T(8,128)(2,1)S(1)}, bf16[16,3200]{1,0:T(8,128)(2,1)S(1)}, u32[]{:S(2)}, u32[]{:S(2)}) collective-permute-start(bf16[16,3200]{1,0:T(8,128)(2,1)S(1)} %join.4.after_ref.own_ref), channel_id=1, source_target_pairs={{0,4},{1,5},{2,6},{3,7},{4,0},{5,1},{6,2},{7,3},{8,12},{9,13},{10,... | collective-permute-start | bytes 307208 | tf_op jit(solution)/shard_map/ppermute | solution.py:411
  14.0 6.3 %collective-permute-start.2 = (bf16[32,3200]{1,0:T(8,128)(2,1)S(1)}, bf16[32,3200]{1,0:T(8,128)(2,1)S(1)}, u32[]{:S(2)}, u32[]{:S(2)}) collective-permute-start(bf16[32,3200]{1,0:T(8,128)(2,1)S(1)} %join.5.source_ref.after_ref), channel_id=1, source_target_pairs={{0,2},{1,3},{2,0},{3,1},{4,6},{5,7},{6,4},{7,5},{8,10},{9,11},{10,... | collective-permute-start | bytes 614408 | tf_op jit(solution)/shard_map/ppermute | solution.py:411
  15.8 6.4 %slice-start.2 = ((s8[12582912]{0:T(1024)(128)(4,1)}), s8[4194304]{0:T(1024)(128)(4,1)S(1)}, s32[]{:S(2)}) async-start(s8[12582912]{0:T(1024)(128)(4,1)} %bitcast.14), calls=%async_computation.3 | async-start | bytes 8388608
  15.8 4.7 %collective-permute-start.3 = (bf16[16,3200]{1,0:T(8,128)(2,1)S(1)}, bf16[16,3200]{1,0:T(8,128)(2,1)S(1)}, u32[]{:S(2)}, u32[]{:S(2)}) collective-permute-start(bf16[16,3200]{1,0:T(8,128)(2,1)S(1)} %select.6.own_ref), channel_id=1, source_target_pairs={{0,16},{1,17},{2,18},{3,19},{4,20},{5,21},{6,22},{7,23},{8,24},{9,... | collective-permute-start | bytes 307208 | tf_op jit(solution)/shard_map/ppermute | solution.py:411
  20.6 1.6 %collective-permute-start.4 = (bf16[32,3200]{1,0:T(8,128)(2,1)S(1)}, bf16[32,3200]{1,0:T(8,128)(2,1)S(1)}, u32[]{:S(2)}, u32[]{:S(2)}) collective-permute-start(bf16[32,3200]{1,0:T(8,128)(2,1)S(1)} %join.6.refs_0_), channel_id=1, source_target_pairs={{0,1},{1,0},{2,3},{3,2},{4,5},{5,4},{6,7},{7,6},{8,9},{9,8},{10,11... | collective-permute-start | bytes 614408 | tf_op jit(solution)/shard_map/ppermute | solution.py:411
  20.7 6.0 %collective-permute-start.5 = (bf16[16,3200]{1,0:T(8,128)(2,1)S(1)}, bf16[16,3200]{1,0:T(8,128)(2,1)S(1)}, u32[]{:S(2)}, u32[]{:S(2)}) collective-permute-start(bf16[16,3200]{1,0:T(8,128)(2,1)S(1)} %select.7.got_ref), channel_id=1, source_target_pairs={{0,16},{1,17},{2,18},{3,19},{4,20},{5,21},{6,22},{7,23},{8,24},{9,... | collective-permute-start | bytes 307208 | tf_op jit(solution)/shard_map/ppermute | solution.py:411
  22.3 4.7 %copy-start.1 = (s32[8,2]{0,1:T(2,128)S(1)}, s32[8,2]{0,1:T(2,128)}, u32[]{:S(2)}) copy-start(s32[8,2]{0,1:T(2,128)} %param.10) | copy-start | bytes 196
  26.7 1.5 %collective-permute-start.6 = (bf16[32,3200]{1,0:T(8,128)(2,1)S(1)}, bf16[32,3200]{1,0:T(8,128)(2,1)S(1)}, u32[]{:S(2)}, u32[]{:S(2)}) collective-permute-start(bf16[32,3200]{1,0:T(8,128)(2,1)S(1)} %join.7.refs_2_), channel_id=1, source_target_pairs={{0,1},{1,0},{2,3},{3,2},{4,5},{5,4},{6,7},{7,6},{8,9},{9,8},{10,11... | collective-permute-start | bytes 614408 | tf_op jit(solution)/shard_map/ppermute | solution.py:411
  37.0 9.2 %collective-permute-start.7 = (bf16[784,128]{1,0:T(8,128)(2,1)S(1)}, bf16[784,128]{1,0:T(8,128)(2,1)S(1)}, u32[]{:S(2)}, u32[]{:S(2)}) collective-permute-start(bf16[784,128]{1,0:T(8,128)(2,1)S(1)} %back_other.1), channel_id=1, source_target_pairs={{0,16},{1,17},{2,18},{3,19},{4,20},{5,21},{6,22},{7,23},{8,24},{9,... | collective-permute-start | bytes 602120 | tf_op jit(solution)/shard_map/ppermute | solution.py:411
  47.3 14.2 %all-to-all-start = ((bf16[16,8,896]{2,1,0:T(8,128)(2,1)}), bf16[16,8,896]{2,1,0:T(8,128)(2,1)S(1)}, u32[]{:S(2)}, u32[]{:S(2)}) async-start(bf16[16,8,896]{2,1,0:T(8,128)(2,1)} %bitcast.8), calls=%async_computation | async-start | bytes 458752 | tf_op jit(solution)/shard_map/all_to_all | solution.py:527
